TPU v7x, 512 devices: a whole 4x4x16 slice. The times are simulated.
512 devices in a mesh: leaf: 32 (over z, core), blk: 16 (over y, x).
Axes of the slice: x: 4, y: 4, z: 16, core: 2. Of those that a mesh axis runs over, the one named last changes fastest.
Arguments:
- rhs_local: float32 [262144, 32], P(('leaf', 'blk')), may hold values from -6 to 6
- inv_local: float32 [262144, 512], P(('leaf', 'blk'))
- couple_local: float32 [262144, 1536], P(('leaf', 'blk')), may hold values from -0.02734375 to 0.02734375
- row_index: int32 [512, 1536], P(('leaf', 'blk')), may hold values from 0 to 8191, as said below
- rhs_sep1: float32 [8192, 32], P(('leaf', 'blk')), may hold values from -6 to 6
- inv_sep1: float32 [8192, 4096], P(('leaf', 'blk'))
- couple_sep1: float32 [8192, 4096], P(('leaf', 'blk')), may hold values from -0.0625 to 0.0625
- rhs_sep0: float32 [4096, 32], P(('leaf', 'blk')), may hold values from -6 to 6
- inv_sep0: float32 [4096, 4096], P(('leaf', 'blk'))
Outputs:
- x_local: float32 [262144, 32], P(('leaf', 'blk'))
- x_sep1: float32 [8192, 32], P(('leaf', 'blk'))
- x_sep0: float32 [4096, 32], P(('leaf', 'blk'))
Inputs may be any that keep to these rules, and one draw needn't show every extreme that they name: `row_index`: row d lists 1536 distinct rows in increasing order among the 8192 rows of device-local supernode d's ancestors (its level-1 separator, then the root, 4096 rows each); it always holds the first and the last of them.
All inputs are finite; a program needn't handle non-finite values.
Results may differ from a plain program's by a relative error of at most 0.00013.
Values sent between devices are 32-bit elements; how exact they have to be, the bound alone decides.
No kernel may reach another device: no remote copies, remote signals or barrier semaphores. Data moves between devices by JAX's collectives and lax.ppermute only.
A program may use at most 64 MiB of HBM per device.

v0:
```python
import jax
import jax.numpy as jnp
from jax import lax
from jax.sharding import PartitionSpec as P


def from_partner(value, axis, distance):
    mask = 2**distance
    pairs = [(source, source ^ mask) for source in range(lax.axis_size(axis))]
    return lax.ppermute(value, axis, pairs)


def group_total(partial_value, leaf_bits):
    summed = lax.psum_scatter(partial_value, "blk", scatter_dimension=0, tiled=True)
    for level_bit in range(leaf_bits):
        summed = summed + from_partner(summed, "leaf", level_bit)
    return lax.all_gather(summed, "blk", axis=0, tiled=True)


def root_total(partial_value, leaf_bits):
    return group_total(partial_value, leaf_bits)


def place_rows(negated, own_rows, offset):
    current = lax.dynamic_slice_in_dim(negated, offset, own_rows.shape[0], 0)
    return lax.dynamic_update_slice_in_dim(negated, current + own_rows, offset, 0)


def matmul(left, right):
    return jnp.dot(left, right, precision=lax.Precision.HIGHEST, preferred_element_type=jnp.float32)


def shards(
    rhs_local,
    inv_local,
    couple_local,
    row_index,
    rhs_sep1,
    inv_sep1,
    couple_sep1,
    rhs_sep0,
    inv_sep0,
):
    leaf_count = lax.axis_size("leaf")
    blk_count = lax.axis_size("blk")
    all_devices = leaf_count * blk_count
    leaf_bits = leaf_count.bit_length() - 1
    flat_index = lax.axis_index("leaf") * blk_count + lax.axis_index("blk")
    sep_rows = inv_sep0.shape[1]
    offset_one = flat_index % (all_devices // 2) * rhs_sep1.shape[0]
    offset_root = flat_index * rhs_sep0.shape[0]
    solved_local = matmul(inv_local, rhs_local)
    lifted = matmul(couple_local.T, solved_local)
    update = jnp.zeros((2 * sep_rows, rhs_local.shape[1]), jnp.float32).at[row_index[0]].add(lifted)
    right_one = group_total(place_rows(-update[:sep_rows], rhs_sep1, offset_one), leaf_bits - 1)
    solved_one = matmul(inv_sep1, right_one)
    update_root = update[sep_rows:] + matmul(couple_sep1.T, solved_one)
    right_root = root_total(place_rows(-update_root, rhs_sep0, offset_root), leaf_bits)
    solved_root = matmul(inv_sep0, right_root)
    x_root = root_total(matmul(inv_sep0.T, solved_root), leaf_bits)
    rest_one = solved_one - matmul(couple_sep1, x_root)
    x_one = group_total(matmul(inv_sep1.T, rest_one), leaf_bits - 1)
    ancestor = jnp.concatenate([x_one, x_root], axis=0)
    rest_local = solved_local - matmul(couple_local, ancestor[row_index[0]])
    x_local = matmul(inv_local.T, rest_local)
    own_one = lax.dynamic_slice_in_dim(x_one, offset_one, rhs_sep1.shape[0], 0)
    own_root = lax.dynamic_slice_in_dim(x_root, offset_root, rhs_sep0.shape[0], 0)
    return (x_local, own_one, own_root)


def solution(mesh):
    in_specs = (
        P(("leaf", "blk"), None),
        P(("leaf", "blk"), None),
        P(("leaf", "blk"), None),
        P(("leaf", "blk"), None),
        P(("leaf", "blk"), None),
        P(("leaf", "blk"), None),
        P(("leaf", "blk"), None),
        P(("leaf", "blk"), None),
        P(("leaf", "blk"), None),
    )
    out_specs = (P(("leaf", "blk"), None), P(("leaf", "blk"), None), P(("leaf", "blk"), None))
    return jax.shard_map(shards, mesh=mesh, in_specs=in_specs, out_specs=out_specs, check_vma=False)
```

profile of v0, /device:TPU:1, one launch (start us, length us, event | category | flops | bytes accessed | tf_op | source)
XLA Modules:
  0.0 662.0 jit_solution(11327609233446967032)
XLA Ops:
  13.5 11.3 %scatter_custom_fusion = f32[8192,32]{1,0:T(8,128)} fusion(s32[1536]{0:T(1024)S(1)} %fusion.5, f32[1536,32]{1,0:T(8,128)} %copy.18, f32[]{:T(128)} %constant.11.clone.1), kind=kCustom, calls=%fused_computation.9 | custom fusion | flops 49152 | bytes 1049088 | tf_op jit(solution)/shard_map/scatter-add | solution.py:54
  24.8 4.5 slice_negate_fusion
  30.7 93.4 %reduce-scatter.5.cloned.1.call-done = f32[256,32]{1,0:T(8,128)} async-done(((f32[4096,32]{1,0:T(8,128)}), f32[256,32]{1,0:T(8,128)}) %reduce-scatter.5.cloned.1.call-update) | async-done | bytes 32784 | tf_op jit(solution)/shard_map/reduce_scatter | solution.py:14
  124.1 4.2 collective-permute-start
  130.4 3.2 collective-permute-start.1
  133.6 3.4 collective-permute-done.1
  137.1 4.2 collective-permute-start.2
  141.3 5.8 collective-permute-done.2
  147.7 7.3 %collective-permute-start.3 = (f32[256,32]{1,0:T(8,128)}, f32[256,32]{1,0:T(8,128)}, u32[]{:S(2)}, u32[]{:S(2)}) collective-permute-start(f32[256,32]{1,0:T(8,128)} %add.108), channel_id=1, source_target_pairs={{0,128},{16,144},{32,160},{48,176},{64,192},{80,208},{96,224},{112... | collective-permute-start | bytes 98312 | tf_op jit(solution)/shard_map/ppermute | solution.py:10
  158.1 7.7 %collective-permute-done.3 = f32[256,32]{1,0:T(8,128)} collective-permute-done((f32[256,32]{1,0:T(8,128)}, f32[256,32]{1,0:T(8,128)}, u32[]{:S(2)}, u32[]{:S(2)}) %collective-permute-start.3) | collective-permute-done | bytes 32800 | tf_op jit(solution)/shard_map/ppermute | solution.py:10
  166.8 21.9 %all_gather.12 = f32[4096,32]{1,0:T(8,128)S(1)} all-gather(f32[256,32]{1,0:T(8,128)S(1)} %add.109), channel_id=1, replica_groups=mesh['leaf'=32,'blk'=16] {'blk'}, dimensions={0}, use_global_device_ids=true | all-gather | bytes 557056 | tf_op jit(solution)/shard_map/all_gather | solution.py:17
  193.9 89.2 %reduce-scatter.7.cloned.1.call-done = f32[256,32]{0,1:T(8,128)} async-done(((f32[4096,32]{0,1:T(8,128)}), f32[256,32]{0,1:T(8,128)}) %reduce-scatter.7.cloned.1.call-update) | async-done | bytes 32784 | tf_op jit(solution)/shard_map/reduce_scatter | solution.py:14
  283.1 4.2 collective-permute-start.4
  293.8 4.2 collective-permute-start.6
  299.3 7.4 %collective-permute-start.7 = (f32[256,32]{0,1:T(8,128)S(1)}, f32[256,32]{0,1:T(8,128)S(1)}, u32[]{:S(2)}, u32[]{:S(2)}) collective-permute-start(f32[256,32]{0,1:T(8,128)S(1)} %add.115), channel_id=1, source_target_pairs={{0,128},{16,144},{32,160},{48,176},{64,192},{80,208},{96,224},{112... | collective-permute-start | bytes 98312 | tf_op jit(solution)/shard_map/ppermute | solution.py:10
  308.0 13.6 %collective-permute-start.8 = (f32[256,32]{0,1:T(8,128)S(1)}, f32[256,32]{0,1:T(8,128)S(1)}, u32[]{:S(2)}, u32[]{:S(2)}) collective-permute-start(f32[256,32]{0,1:T(8,128)S(1)} %add.116), channel_id=1, source_target_pairs={{0,256},{16,272},{32,288},{48,304},{64,320},{80,336},{96,352},{112... | collective-permute-start | bytes 98312 | tf_op jit(solution)/shard_map/ppermute | solution.py:10
  322.9 17.8 %all_gather.13 = f32[4096,32]{0,1:T(8,128)S(1)} all-gather(f32[256,32]{0,1:T(8,128)S(1)} %add.117), channel_id=1, replica_groups=mesh['leaf'=32,'blk'=16] {'blk'}, dimensions={0}, use_global_device_ids=true | all-gather | bytes 557056 | tf_op jit(solution)/shard_map/all_gather | solution.py:17
  344.5 94.3 %reduce-scatter.9.cloned.1.call-done = f32[256,32]{0,1:T(8,128)} async-done(((f32[4096,32]{0,1:T(8,128)}), f32[256,32]{0,1:T(8,128)}) %reduce-scatter.9.cloned.1.call-update) | async-done | bytes 32784 | tf_op jit(solution)/shard_map/reduce_scatter | solution.py:14
  438.8 4.2 collective-permute-start.9
  444.8 3.2 collective-permute-start.10
  449.4 4.1 collective-permute-start.11
  455.0 7.4 %collective-permute-start.12 = (f32[256,32]{0,1:T(8,128)S(1)}, f32[256,32]{0,1:T(8,128)S(1)}, u32[]{:S(2)}, u32[]{:S(2)}) collective-permute-start(f32[256,32]{0,1:T(8,128)S(1)} %add.120), channel_id=1, source_target_pairs={{0,128},{16,144},{32,160},{48,176},{64,192},{80,208},{96,224},{112... | collective-permute-start | bytes 98312 | tf_op jit(solution)/shard_map/ppermute | solution.py:10
  463.6 13.7 %collective-permute-start.13 = (f32[256,32]{0,1:T(8,128)S(1)}, f32[256,32]{0,1:T(8,128)S(1)}, u32[]{:S(2)}, u32[]{:S(2)}) collective-permute-start(f32[256,32]{0,1:T(8,128)S(1)} %add.121), channel_id=1, source_target_pairs={{0,256},{16,272},{32,288},{48,304},{64,320},{80,336},{96,352},{112... | collective-permute-start | bytes 98312 | tf_op jit(solution)/shard_map/ppermute | solution.py:10
  478.6 18.0 %all_gather.14 = f32[4096,32]{0,1:T(8,128)S(1)} all-gather(f32[256,32]{0,1:T(8,128)S(1)} %add.122), channel_id=1, replica_groups=mesh['leaf'=32,'blk'=16] {'blk'}, dimensions={0}, use_global_device_ids=true | all-gather | bytes 557056 | tf_op jit(solution)/shard_map/all_gather | solution.py:17
  500.3 94.3 %reduce-scatter.11.cloned.1.call-done = f32[256,32]{0,1:T(8,128)} async-done(((f32[4096,32]{0,1:T(8,128)}), f32[256,32]{0,1:T(8,128)}) %reduce-scatter.11.cloned.1.call-update) | async-done | bytes 32784 | tf_op jit(solution)/shard_map/reduce_scatter | solution.py:14
  594.6 4.2 collective-permute-start.14
  605.3 4.1 collective-permute-start.16
  610.8 7.3 %collective-permute-start.17 = (f32[256,32]{0,1:T(8,128)S(1)}, f32[256,32]{0,1:T(8,128)S(1)}, u32[]{:S(2)}, u32[]{:S(2)}) collective-permute-start(f32[256,32]{0,1:T(8,128)S(1)} %add.125), channel_id=1, source_target_pairs={{0,128},{16,144},{32,160},{48,176},{64,192},{80,208},{96,224},{112... | collective-permute-start | bytes 98312 | tf_op jit(solution)/shard_map/ppermute | solution.py:10
  619.6 17.8 %all_gather.15 = f32[4096,32]{0,1:T(8,128)S(1)} all-gather(f32[256,32]{0,1:T(8,128)S(1)} %add.126), channel_id=1, replica_groups=mesh['leaf'=32,'blk'=16] {'blk'}, dimensions={0}, use_global_device_ids=true | all-gather | bytes 557056 | tf_op jit(solution)/shard_map/all_gather | solution.py:17
  639.6 3.6 copy.21
  643.2 5.9 gather_fusion
  649.1 4.3 fusion.4
  (81 shorter events, 58.3 us)
Async XLA Ops:
  7.2 3.3 copy-start
  7.2 116.9 %reduce-scatter.5.cloned.1.call-start = ((), (), s32[]{:S(2)}) async-start(), calls=%async_computation.4 | async-start | bytes 2228224 | tf_op jit(solution)/shard_map/reduce_scatter | solution.py:14
  24.8 4.5 copy-start.6
  29.3 128.7 %copy-start.7 = (f32[8,32]{1,0:T(8,128)S(1)}, f32[8,32]{1,0:T(8,128)}, u32[]{:S(2)}) copy-start(f32[8,32]{1,0:T(8,128)} %param.16) | copy-start | bytes 3076
  30.6 252.5 %reduce-scatter.7.cloned.1.call-start = ((), (), s32[]{:S(2)}) async-start(), calls=%async_computation.5 | async-start | bytes 557056 | tf_op jit(solution)/shard_map/reduce_scatter | solution.py:14
  124.1 5.4 collective-permute-start
  130.4 6.6 collective-permute-start.1
  137.1 10.0 %collective-permute-start.2 = (f32[256,32]{1,0:T(8,128)S(1)}, f32[256,32]{1,0:T(8,128)S(1)}, u32[]{:S(2)}, u32[]{:S(2)}) collective-permute-start(f32[256,32]{1,0:T(8,128)S(1)} %add.107), channel_id=1, source_target_pairs={{0,64},{16,80},{32,96},{48,112},{64,0},{80,16},{96,32},{112,48},{1... | collective-permute-start | bytes 98312 | tf_op jit(solution)/shard_map/ppermute | solution.py:10
  147.7 18.1 %collective-permute-start.3 = (f32[256,32]{1,0:T(8,128)}, f32[256,32]{1,0:T(8,128)}, u32[]{:S(2)}, u32[]{:S(2)}) collective-permute-start(f32[256,32]{1,0:T(8,128)} %add.108), channel_id=1, source_target_pairs={{0,128},{16,144},{32,160},{48,176},{64,192},{80,208},{96,224},{112... | collective-permute-start | bytes 98312 | tf_op jit(solution)/shard_map/ppermute | solution.py:10
  158.0 32.9 %copy-start.5 = (f32[16,4096]{1,0:T(8,128)S(1)}, f32[16,4096]{1,0:T(8,128)}, u32[]{:S(2)}) copy-start(f32[16,4096]{1,0:T(8,128)} %param.15) | copy-start | bytes 786436
  158.1 32.8 %copy-start.4 = (f32[4096,32]{0,1:T(8,128)S(1)}, f32[4096,32]{0,1:T(8,128)}, u32[]{:S(2)}) copy-start(f32[4096,32]{0,1:T(8,128)} %copy.24) | copy-start | bytes 1572868
  191.5 0.8 copy-start.3
  193.8 245.0 %reduce-scatter.9.cloned.1.call-start = ((), (), s32[]{:S(2)}) async-start(), calls=%async_computation.6 | async-start | bytes 557056 | tf_op jit(solution)/shard_map/reduce_scatter | solution.py:14
  283.1 5.2 collective-permute-start.4
  289.1 4.6 collective-permute-start.5
  293.8 5.5 collective-permute-start.6
  299.3 8.7 %collective-permute-start.7 = (f32[256,32]{0,1:T(8,128)S(1)}, f32[256,32]{0,1:T(8,128)S(1)}, u32[]{:S(2)}, u32[]{:S(2)}) collective-permute-start(f32[256,32]{0,1:T(8,128)S(1)} %add.115), channel_id=1, source_target_pairs={{0,128},{16,144},{32,160},{48,176},{64,192},{80,208},{96,224},{112... | collective-permute-start | bytes 98312 | tf_op jit(solution)/shard_map/ppermute | solution.py:10
  308.0 14.9 %collective-permute-start.8 = (f32[256,32]{0,1:T(8,128)S(1)}, f32[256,32]{0,1:T(8,128)S(1)}, u32[]{:S(2)}, u32[]{:S(2)}) collective-permute-start(f32[256,32]{0,1:T(8,128)S(1)} %add.116), channel_id=1, source_target_pairs={{0,256},{16,272},{32,288},{48,304},{64,320},{80,336},{96,352},{112... | collective-permute-start | bytes 98312 | tf_op jit(solution)/shard_map/ppermute | solution.py:10
  344.5 250.1 %reduce-scatter.11.cloned.1.call-start = ((), (), s32[]{:S(2)}) async-start(), calls=%async_computation.7 | async-start | bytes 557056 | tf_op jit(solution)/shard_map/reduce_scatter | solution.py:14
  438.8 5.2 collective-permute-start.9
  444.8 4.6 collective-permute-start.10
  449.4 5.5 collective-permute-start.11
  455.0 8.6 %collective-permute-start.12 = (f32[256,32]{0,1:T(8,128)S(1)}, f32[256,32]{0,1:T(8,128)S(1)}, u32[]{:S(2)}, u32[]{:S(2)}) collective-permute-start(f32[256,32]{0,1:T(8,128)S(1)} %add.120), channel_id=1, source_target_pairs={{0,128},{16,144},{32,160},{48,176},{64,192},{80,208},{96,224},{112... | collective-permute-start | bytes 98312 | tf_op jit(solution)/shard_map/ppermute | solution.py:10
  463.6 15.0 %collective-permute-start.13 = (f32[256,32]{0,1:T(8,128)S(1)}, f32[256,32]{0,1:T(8,128)S(1)}, u32[]{:S(2)}, u32[]{:S(2)}) collective-permute-start(f32[256,32]{0,1:T(8,128)S(1)} %add.121), channel_id=1, source_target_pairs={{0,256},{16,272},{32,288},{48,304},{64,320},{80,336},{96,352},{112... | collective-permute-start | bytes 98312 | tf_op jit(solution)/shard_map/ppermute | solution.py:10
  496.6 0.8 copy-start.1
  594.6 5.3 collective-permute-start.14
  600.6 4.6 collective-permute-start.15
  605.3 5.5 collective-permute-start.16
  610.8 8.8 %collective-permute-start.17 = (f32[256,32]{0,1:T(8,128)S(1)}, f32[256,32]{0,1:T(8,128)S(1)}, u32[]{:S(2)}, u32[]{:S(2)}) collective-permute-start(f32[256,32]{0,1:T(8,128)S(1)} %add.125), channel_id=1, source_target_pairs={{0,128},{16,144},{32,160},{48,176},{64,192},{80,208},{96,224},{112... | collective-permute-start | bytes 98312 | tf_op jit(solution)/shard_map/ppermute | solution.py:10
  649.1 4.3 copy-start.2
Sparse Core Ops, SparseCore 0:
  30.7 93.3 reduce-scatter.4
  193.9 89.1 reduce-scatter.6
  344.6 94.1 reduce-scatter.8
  500.4 94.1 reduce-scatter.10
where the time goes:
time: 670 us; the launch traced here: 662 us
  waiting for transfers between devices  406 us (61%)
  starting transfers between devices  103 us (15%)
  blocking collectives  75.5 us (11%)
  other arithmetic  25.1 us (4%)
  matrix products  19.3 us (3%)
  local copies, waits for them, and re-layouts  18.9 us (3%)
  between operations  14.1 us (2%)
    reduce_scatter x4, waiting for transfers between devices, group_total(): lax.psum_scatter(partial_value, 'blk', scatter_dimension=0, tiled=True)  371 us
    ppermute x18, starting transfers between devices, from_partner(): return lax.ppermute(value, axis, pairs)  103 us
    all_gather x4, blocking collectives, group_total(): return lax.all_gather(summed, 'blk', axis=0, tiled=True)  75.5 us
    ppermute x18, waiting for transfers between devices, from_partner(): return lax.ppermute(value, axis, pairs)  35 us
    dot_general x10, matrix products, matmul(): jnp.dot(left, right, precision=lax.Precision.HIGHEST, preferred_element_t...  19.3 us
  transfers between devices with their start and end apart: 22, of which 21 were waited for; matrix products, arithmetic and copies ran while one was open for 1% of the time, Pallas kernels for 0%

commit v1 on v0

v1 whole, which is shorter than its diff:
```python
import jax
import jax.numpy as jnp
from jax import lax
from jax.sharding import Mesh
from jax.sharding import PartitionSpec as P

HIGHEST = lax.Precision.HIGHEST
PLANE = ("core", "blk")
HALF = ("plane",)
LINE = ("half", "plane")


def product(left, right, left_dim, right_dim):
    dims = (((left_dim,), (right_dim,)), ((), ()))
    return lax.dot_general(left, right, dims, precision=HIGHEST, preferred_element_type=jnp.float32)


def exchange(slots, axes):
    return lax.all_to_all(slots, axes, 0, 0)


def spread(value, axes):
    return exchange(jnp.broadcast_to(value[None], (lax.axis_size(axes),) + value.shape), axes)


def total(value, axes):
    return jnp.sum(spread(value, axes), axis=0)


def by_member(wide, members):
    rows, columns = wide.shape
    return wide.reshape(rows, members, columns // members).transpose(1, 0, 2)


def side_by_side(stacked):
    members, rows, columns = stacked.shape
    return stacked.transpose(1, 0, 2).reshape(rows, members * columns)


def place_rows(values, own_rows, offset):
    current = lax.dynamic_slice_in_dim(values, offset, own_rows.shape[0], 0)
    return lax.dynamic_update_slice_in_dim(values, current + own_rows, offset, 0)


def shards(
    rhs_local,
    inv_local,
    couple_local,
    row_index,
    rhs_sep1,
    inv_sep1,
    couple_sep1,
    rhs_sep0,
    inv_sep0,
):
    sep_rows = inv_sep0.shape[1]
    samples = rhs_local.shape[1]
    rows_one = rhs_sep1.shape[0]
    rows_root = rhs_sep0.shape[0]
    members = lax.axis_size(PLANE)
    flat_index = lax.axis_index(("half", "plane", "core", "blk"))
    all_devices = lax.axis_size(("half", "plane", "core", "blk"))
    offset_one = flat_index % (all_devices // 2) * rows_one
    offset_root = flat_index * rows_root

    solved_local = product(rhs_local, inv_local, 0, 1)
    lifted = product(couple_local, solved_local, 0, 1)
    negated = jnp.zeros((2 * sep_rows, samples), jnp.float32).at[row_index[0]].add(-lifted)
    negated = place_rows(negated, rhs_sep1, offset_one)
    negated = place_rows(negated, rhs_sep0, sep_rows + offset_root)
    negated = negated.T

    slots = jnp.concatenate(
        [by_member(negated[:, :sep_rows], members), by_member(inv_sep1, members), by_member(inv_sep0, members)],
        axis=1,
    )
    slots = exchange(slots, PLANE)
    columns = slots.shape[2]
    inv_one = slots[:, samples : samples + rows_one].reshape(members * rows_one, columns)
    inv_root = slots[:, samples + rows_one :].reshape(members * rows_root, columns)

    right_one = total(jnp.sum(slots[:, :samples], axis=0), HALF)
    solved_one = product(inv_one, right_one, 1, 1)
    solved_one = jnp.sum(exchange(solved_one.reshape(members, rows_one, samples), PLANE), axis=0)

    right_root = negated[:, sep_rows:] - product(solved_one, couple_sep1, 0, 0)
    right_root = jnp.sum(exchange(by_member(right_root, members), PLANE), axis=0)
    right_root = total(right_root, LINE)
    solved_root = total(product(right_root, inv_root, 1, 1), PLANE)
    x_root = total(product(solved_root, inv_root, 1, 0), LINE)
    x_root = side_by_side(spread(x_root, PLANE))

    rest_one = solved_one - product(couple_sep1, x_root, 1, 1)
    rest_one = spread(rest_one, PLANE).reshape(members * rows_one, samples)
    x_one = total(product(rest_one, inv_one, 0, 0), HALF)
    x_one = side_by_side(spread(x_one, PLANE))

    ancestor = jnp.concatenate([x_one, x_root], axis=1).T
    rest_local = solved_local - product(ancestor[row_index[0]], couple_local, 0, 1)
    x_local = product(inv_local, rest_local, 0, 1)
    own_one = lax.dynamic_slice_in_dim(ancestor, offset_one, rows_one, 0)
    own_root = lax.dynamic_slice_in_dim(ancestor, sep_rows + offset_root, rows_root, 0)
    return (x_local, own_one, own_root)


def solution(mesh):
    leaf, blk = mesh.devices.shape
    halves = Mesh(mesh.devices.reshape(2, leaf // 4, 2, blk), ("half", "plane", "core", "blk"))
    spec = P(("half", "plane", "core", "blk"), None)
    return jax.shard_map(shards, mesh=halves, in_specs=(spec,) * 9, out_specs=(spec,) * 3, check_vma=False)
```

time: 670 us -> 281 us (0.42); the launches traced: 662 us -> 280 us
  waiting for transfers between devices: 406 us -> 11.2 us
  blocking collectives: 75.5 us -> 188 us
  starting transfers between devices: 103 us -> 6.85 us
  between operations: 14.1 us -> 0.9 us
  local copies, waits for them, and re-layouts: 18.9 us -> 31.5 us
    reduce_scatter x4 -> x0, waiting for transfers between devices: 371 us -> none  [group_total(): lax.psum_scatter(partial_value, 'blk', scatter_dimension=0, tiled=True)]
    all_to_all x0 -> x10, blocking collectives: none -> 188 us  [exchange(): return lax.all_to_all(slots, axes, 0, 0)]
    ppermute x18 -> x0, starting transfers between devices: 103 us -> none  [from_partner(): return lax.ppermute(value, axis, pairs)]
    all_gather x4 -> x0, blocking collectives: 75.5 us -> none  [group_total(): return lax.all_gather(summed, 'blk', axis=0, tiled=True)]
    ppermute x18 -> x0, waiting for transfers between devices: 35 us -> none  [from_partner(): return lax.ppermute(value, axis, pairs)]
    all_to_all x0 -> x1, waiting for transfers between devices: none -> 11.2 us  [exchange(): return lax.all_to_all(slots, axes, 0, 0)]
    all_to_all x0 -> x1, starting transfers between devices: none -> 6.85 us  [exchange(): return lax.all_to_all(slots, axes, 0, 0)]
  transfers between devices with their start and end apart: 22 -> 1, of which waited for: 21 -> 1; matrix products, arithmetic and copies ran while one was open for 1% -> 0% of each run, Pallas kernels for 0% -> 0%
where the time goes in v1:
time: 281 us; the launch traced here: 280 us
  blocking collectives  188 us (67%)
  local copies, waits for them, and re-layouts  31.5 us (11%)
  other arithmetic  23.6 us (8%)
  matrix products  17.8 us (6%)
  waiting for transfers between devices  11.2 us (4%)
  starting transfers between devices  6.85 us (2%)
    all_to_all x10, blocking collectives, exchange(): return lax.all_to_all(slots, axes, 0, 0)  188 us
    dot_general x10, matrix products, product(): lax.dot_general(left, right, dims, precision=HIGHEST, preferred_element_t...  17.8 us
    scatter-add x1, other arithmetic, shards(): jnp.zeros((2 * sep_rows, samples), jnp.float32).at[row_index[0]]  11.3 us
    all_to_all x1, waiting for transfers between devices, exchange(): return lax.all_to_all(slots, axes, 0, 0)  11.2 us
    unnamed x21, local copies, waits for them, and re-layouts  8.84 us
    all_to_all x1, starting transfers between devices, exchange(): return lax.all_to_all(slots, axes, 0, 0)  6.85 us
    gather x1, local copies, waits for them, and re-layouts, shards(): ancestor[row_index[0]]  5.85 us
  transfers between devices with their start and end apart: 1, of which 1 were waited for; matrix products, arithmetic and copies ran while one was open for 0% of the time, Pallas kernels for 0%

profile of v1, /device:TPU:1, one launch (start us, length us, event | category | flops | bytes accessed | tf_op | source)
XLA Modules:
  0.0 279.7 jit_solution(5601237105231530056)
XLA Ops:
  3.1 1.7 bitcast_bitcast_fusion.2
  4.8 2.3 fusion.14
  7.1 1.9 fusion
  9.0 1.2 copy.52
  10.2 11.3 %scatter_custom_fusion = f32[8192,32]{1,0:T(8,128)} fusion(s32[1536]{0:T(1024)S(1)} %fusion.13, f32[1536,32]{1,0:T(8,128)} %copy.52, f32[]{:T(128)} %constant.16.clone.1), kind=kCustom, calls=%fused_computation.5 | custom fusion | flops 49152 | bytes 1049088 | tf_op jit(solution)/shard_map/scatter-add | solution.py:68
  21.4 3.6 %copy.55 = f32[8192,32]{0,1:T(8,128)} copy(f32[8192,32]{1,0:T(8,128)} %scatter_custom_fusion) | data formatting | bytes 2097152 | tf_op jit(solution)/shard_map/scatter-add | solution.py:68
  25.9 1.4 dynamic_update_slice.6
  28.1 1.4 dynamic_update_slice.7
  31.6 24.8 %all_to_all.55 = f32[32,56,128]{2,1,0:T(8,128)S(1)} all-to-all(f32[32,56,128]{2,1,0:T(8,128)S(1)} %pad_maximum_fusion), channel_id=1, replica_groups=mesh['half'=2,'plane'=8,'core'=2,'blk'=16] {'core','blk'}, dimensions={0} | all-to-all | bytes 1835008 | tf_op jit(solution)/shard_map/all_to_all | solution.py:19
  57.4 21.5 %all_to_all.56 = f32[8,32,128]{2,1,0:T(8,128)} all-to-all(f32[8,32,128]{2,1,0:T(8,128)S(1)} %broadcast_in_dim.19), channel_id=1, replica_groups=mesh['half'=2,'plane'=8,'core'=2,'blk'=16] {'plane'}, dimensions={0} | all-to-all | bytes 262144 | tf_op jit(solution)/shard_map/all_to_all | solution.py:19
  79.8 2.0 fusion.8
  81.8 1.1 reshape.96
  83.0 13.5 %all_to_all.57 = f32[32,1,512]{2,1,0:T(1,128)} all-to-all(f32[32,1,512]{2,1,0:T(1,128)S(1)} %reshape.96), channel_id=1, replica_groups=mesh['half'=2,'plane'=8,'core'=2,'blk'=16] {'core','blk'}, dimensions={0} | all-to-all | bytes 131072 | tf_op jit(solution)/shard_map/all_to_all | solution.py:19
  97.0 1.6 reduce.2
  100.4 1.7 fusion.3
  102.1 15.1 %all_to_all.58 = f32[32,32,128]{2,1,0:T(8,128)} all-to-all(f32[32,32,128]{2,1,0:T(8,128)S(1)} %bitcast.84), channel_id=1, replica_groups=mesh['half'=2,'plane'=8,'core'=2,'blk'=16] {'core','blk'}, dimensions={0} | all-to-all | bytes 1048576 | tf_op jit(solution)/shard_map/all_to_all | solution.py:19
  118.4 20.2 %all_to_all.59 = f32[16,32,128]{2,1,0:T(8,128)} all-to-all(f32[16,32,128]{2,1,0:T(8,128)S(1)} %broadcast_in_dim.20), channel_id=1, replica_groups=mesh['half'=2,'plane'=8,'core'=2,'blk'=16] {'half','plane'}, dimensions={0} | all-to-all | bytes 524288 | tf_op jit(solution)/shard_map/all_to_all | solution.py:19
  139.6 1.1 fusion.11
  140.8 26.7 %all_to_all.60 = f32[32,32,256]{2,1,0:T(8,128)} all-to-all(f32[32,32,256]{2,1,0:T(8,128)S(1)} %broadcast_in_dim.21), channel_id=1, replica_groups=mesh['half'=2,'plane'=8,'core'=2,'blk'=16] {'core','blk'}, dimensions={0} | all-to-all | bytes 2097152 | tf_op jit(solution)/shard_map/all_to_all | solution.py:19
  167.5 1.3 reduce_sum.77
  168.8 1.1 fusion.10
  170.0 18.2 %all_to_all.61 = f32[16,32,128]{2,1,0:T(8,128)} all-to-all(f32[16,32,128]{2,1,0:T(8,128)S(1)} %broadcast_in_dim.22), channel_id=1, replica_groups=mesh['half'=2,'plane'=8,'core'=2,'blk'=16] {'half','plane'}, dimensions={0} | all-to-all | bytes 524288 | tf_op jit(solution)/shard_map/all_to_all | solution.py:19
  189.2 21.2 %all_to_all.62 = f32[32,32,128]{2,1,0:T(8,128)S(1)} all-to-all(f32[32,32,128]{2,1,0:T(8,128)S(1)} %broadcast_in_dim.23), channel_id=1, replica_groups=mesh['half'=2,'plane'=8,'core'=2,'blk'=16] {'core','blk'}, dimensions={0} | all-to-all | bytes 1048576 | tf_op jit(solution)/shard_map/all_to_all | solution.py:19
  211.9 11.1 %all_to_all.63 = f32[32,1,512]{2,1,0:T(1,128)S(1)} all-to-all(f32[32,1,512]{2,1,0:T(1,128)S(1)} %reshape.98), channel_id=1, replica_groups=mesh['half'=2,'plane'=8,'core'=2,'blk'=16] {'core','blk'}, dimensions={0} | all-to-all | bytes 131072 | tf_op jit(solution)/shard_map/all_to_all | solution.py:19
  223.9 1.5 convolution_bitcast_fusion.1
  225.4 15.7 %all_to_all.64 = f32[8,32,128]{2,1,0:T(8,128)S(1)} all-to-all(f32[8,32,128]{2,1,0:T(8,128)S(1)} %broadcast_in_dim.25), channel_id=1, replica_groups=mesh['half'=2,'plane'=8,'core'=2,'blk'=16] {'plane'}, dimensions={0} | all-to-all | bytes 262144 | tf_op jit(solution)/shard_map/all_to_all | solution.py:19
  242.0 6.8 %all-to-all-start.10 = ((f32[32,32,128]{2,1,0:T(8,128)}), f32[32,32,128]{2,1,0:T(8,128)}, u32[]{:S(2)}, u32[]{:S(2)}) async-start(f32[32,32,128]{2,1,0:T(8,128)} %broadcast_in_dim.26), calls=%async_computation.10 | async-start | bytes 1048576 | tf_op jit(solution)/shard_map/all_to_all | solution.py:19
  248.9 11.2 %all-to-all-done.10 = f32[32,32,128]{2,1,0:T(8,128)} async-done(((f32[32,32,128]{2,1,0:T(8,128)}), f32[32,32,128]{2,1,0:T(8,128)}, u32[]{:S(2)}, u32[]{:S(2)}) %all-to-all-start.10) | async-done | bytes 524320 | tf_op jit(solution)/shard_map/all_to_all | solution.py:19
  263.3 3.6 %copy.62 = f32[32,8192]{0,1:T(8,128)} copy(f32[32,8192]{1,0:T(8,128)} %copy-done.4) | data formatting | bytes 2097152 | tf_op jit(solution)/shard_map/concatenate | solution.py:98
  268.2 5.9 %gather_fusion = f32[1536,32]{1,0:T(8,128)} fusion(f32[8192,32]{1,0:T(8,128)} %bitcast.81, s32[2048]{0:T(1024)S(1)} %pad_clamp_fusion), kind=kCustom, calls=%fused_computation | custom fusion | bytes 399360 | tf_op jit(solution)/shard_map/gather | solution.py:99
  274.0 4.3 %convolution_subtract_fusion.1 = f32[32,512]{1,0:T(8,128)S(1)} fusion(f32[32,512]{1,0:T(8,128)S(1)} %fusion.14, f32[1536,32]{1,0:T(8,128)} %gather_fusion, f32[512,1536]{1,0:T(8,128)S(1)} %copy-done), kind=kOutput, calls=%fused_computation.9 | convolution fusion | flops 302006272 | bytes 3473408 | tf_op jit(solution)/shard_map/dot_general | solution.py:15
  278.4 1.3 convolution_bitcast_fusion
  (48 shorter events, 21.7 us)
Async XLA Ops:
  0.6 6.5 %copy-start = (f32[512,1536]{1,0:T(8,128)S(1)}, f32[512,1536]{1,0:T(8,128)}, u32[]{:S(2)}) copy-start(f32[512,1536]{1,0:T(8,128)} %param.11) | copy-start | bytes 9437188
  25.1 75.3 %copy-start.5 = (f32[16,4096]{1,0:T(8,128)S(1)}, f32[16,4096]{1,0:T(8,128)}, u32[]{:S(2)}) copy-start(f32[16,4096]{1,0:T(8,128)} %param.15) | copy-start | bytes 786436
  56.4 1.0 copy-start.1
  210.4 0.8 copy-start.2
  242.0 18.0 %all-to-all-start.10 = ((f32[32,32,128]{2,1,0:T(8,128)}), f32[32,32,128]{2,1,0:T(8,128)}, u32[]{:S(2)}, u32[]{:S(2)}) async-start(f32[32,32,128]{2,1,0:T(8,128)} %broadcast_in_dim.26), calls=%async_computation.10 | async-start | bytes 1048576 | tf_op jit(solution)/shard_map/all_to_all | solution.py:19
  262.2 1.0 copy-start.4
  274.0 4.3 %copy-start.3 = (f32[512,512]{1,0:T(8,128)S(1)}, f32[512,512]{1,0:T(8,128)}, u32[]{:S(2)}) copy-start(f32[512,512]{1,0:T(8,128)} %param.10) | copy-start | bytes 3145732

commit v2 on v1

v2 whole, which is shorter than its diff:
```python
import functools

import jax
import jax.numpy as jnp
from jax import lax
from jax.experimental import pallas as pl
from jax.experimental.pallas import tpu as pltpu
from jax.sharding import Mesh
from jax.sharding import PartitionSpec as P

PLANE = ("core", "blk")
HALF = ("plane",)
LINE = ("half", "plane")
EVERY = ("half", "plane", "core", "blk")

VMEM = pl.BlockSpec(memory_space=pltpu.VMEM)
SMEM = pl.BlockSpec(memory_space=pltpu.SMEM)
HBM = pl.BlockSpec(memory_space=pltpu.HBM)
LANES = 128
UNROLL = 16


def halves(value):
    high = value.astype(jnp.bfloat16)
    return high, (value - high.astype(jnp.float32)).astype(jnp.bfloat16)


def dot16(left, right):
    return jnp.dot(left, right, preferred_element_type=jnp.float32)


def tall_product(left, right):
    n = right.shape[1]
    left_high, left_low = halves(left)
    right_high, right_low = halves(right)
    both = dot16(left_high, jnp.concatenate([right_high, right_low], axis=1))
    return both[:, :n] + (both[:, n:] + dot16(left_low, right_high))


def wide_product(left, right):
    m = left.shape[0]
    left_high, left_low = halves(left)
    right_high, right_low = halves(right)
    both = dot16(jnp.concatenate([left_high, left_low], axis=0), right_high)
    return both[:m] + (both[m:] + dot16(left_high, right_low))


def fetch(pairs, sems):
    copies = [pltpu.make_async_copy(source, target, sems.at[k]) for k, (source, target) in enumerate(pairs)]
    for copy in copies:
        copy.start()
    return copies


def own_position(axes):
    position = lax.axis_index(axes[0])
    for axis in axes[1:]:
        position = position * lax.axis_size(axis) + lax.axis_index(axis)
    return position


def forward_kernel(
    position, rhs, inv, couple, index, rhs_one, inv_one, rhs_root, inv_root, slots, root, solved,
    rhs_here, inv_here, couple_here, index_here, rhs_one_here, inv_one_here, rhs_root_here, inv_root_here, update, lifted, sems,
):
    copies = fetch(
        [
            (rhs, rhs_here),
            (inv, inv_here),
            (index, index_here),
            (couple, couple_here),
            (rhs_one, rhs_one_here),
            (rhs_root, rhs_root_here),
            (inv_one, inv_one_here),
            (inv_root, inv_root_here),
        ],
        sems,
    )
    get_rhs, get_inv, get_index, get_couple, get_rhs_one, get_rhs_root, get_inv_one, get_inv_root = copies
    samples = rhs.shape[0]
    count = index.shape[1]
    rows_one = rhs_one.shape[0]
    rows_root = rhs_root.shape[0]
    sep_rows = inv_one.shape[1]
    members = slots.shape[0]

    @pl.loop(0, update.shape[0] // 512)
    def _(step):
        update[pl.ds(pl.multiple_of(step * 512, 512), 512), :] = jnp.zeros((512, samples), jnp.float32)

    get_rhs.wait()
    get_inv.wait()
    y = tall_product(inv_here[...], rhs_here[...].T)
    solved[...] = y
    y = -y.T
    get_couple.wait()
    step = couple_here.shape[1] // 2
    for start in range(0, couple_here.shape[1], step):
        lifted[start : start + step, :] = wide_product(y, couple_here[:, start : start + step]).T

    get_index.wait()

    @pl.loop(0, count // UNROLL)
    def _(step):
        base = pl.multiple_of(step * UNROLL, UNROLL)
        for k in range(UNROLL):
            update[pl.ds(index_here[0, base + k], 1), :] = lifted[pl.ds(base + k, 1), :]

    get_rhs_one.wait()
    get_rhs_root.wait()
    here = position()
    own_one = pl.ds(pl.multiple_of(here % (sep_rows // rows_one) * rows_one, rows_one), rows_one)
    update[own_one, :] = update[own_one, :] + rhs_one_here[...]
    own_root = pl.ds(pl.multiple_of(sep_rows + here * rows_root, rows_root), rows_root)
    update[own_root, :] = update[own_root, :] + rhs_root_here[...]

    group = LANES // samples
    for first in range(0, 2 * members, group):
        packed = jnp.concatenate([update[(first + g) * LANES : (first + g + 1) * LANES, :] for g in range(group)], axis=1).T
        for g in range(group):
            piece = packed[g * samples : (g + 1) * samples]
            if first < members:
                slots[first + g, :samples, :] = piece
            else:
                root[first + g - members] = piece

    get_inv_one.wait()
    get_inv_root.wait()
    for member in range(members):
        columns = slice(member * LANES, (member + 1) * LANES)
        slots[member, samples : samples + rows_one, :] = inv_one_here[:, columns]
        slots[member, samples + rows_one :, :] = inv_root_here[:, columns]


def forward(rhs_local, inv_local, couple_local, row_index, rhs_sep1, inv_sep1, rhs_sep0, inv_sep0, position):
    samples = rhs_local.shape[1]
    members = inv_sep1.shape[1] // LANES
    slot_rows = samples + inv_sep1.shape[0] + inv_sep0.shape[0]
    given = (rhs_local.T, inv_local, couple_local, row_index, rhs_sep1, inv_sep1, rhs_sep0, inv_sep0)
    here = [pltpu.VMEM(array.shape, array.dtype) for array in given]
    here[3] = pltpu.SMEM(row_index.shape, row_index.dtype)
    return pl.pallas_call(
        functools.partial(forward_kernel, position),
        out_shape=(
            jax.ShapeDtypeStruct((members, slot_rows, LANES), jnp.float32),
            jax.ShapeDtypeStruct((members, samples, LANES), jnp.float32),
            jax.ShapeDtypeStruct(rhs_local.shape, jnp.float32),
        ),
        in_specs=[HBM] * len(given),
        out_specs=(VMEM, VMEM, VMEM),
        scratch_shapes=here
        + [
            pltpu.VMEM((2 * inv_sep1.shape[1], samples), jnp.float32),
            pltpu.VMEM((couple_local.shape[1], samples), jnp.float32),
            pltpu.SemaphoreType.DMA((len(given),)),
        ],
        compiler_params=pltpu.CompilerParams(vmem_limit_bytes=63 * 2**20),
        name="local_forward",
    )(*given)


def backward_kernel(
    position, one, root, solved, inv, couple, index, x_local, own_one, own_root,
    inv_here, couple_here, index_here, ancestor, above, sems,
):
    get_index, get_couple, get_inv = fetch([(index, index_here), (couple, couple_here), (inv, inv_here)], sems)
    samples = solved.shape[1]
    count = index.shape[1]
    members = one.shape[0]
    sep_rows = members * LANES
    group = LANES // samples
    for first in range(0, 2 * members, group):
        source = one if first < members else root
        start = first % members
        packed = source[start : start + group].reshape(LANES, LANES).T
        for g in range(group):
            ancestor[(first + g) * LANES : (first + g + 1) * LANES, :] = packed[:, g * samples : (g + 1) * samples]

    here = position()
    rows_one = own_one.shape[0]
    rows_root = own_root.shape[0]
    own_one[...] = ancestor[pl.ds(pl.multiple_of(here % (sep_rows // rows_one) * rows_one, rows_one), rows_one), :]
    own_root[...] = ancestor[pl.ds(pl.multiple_of(sep_rows + here * rows_root, rows_root), rows_root), :]
    get_index.wait()

    @pl.loop(0, count // UNROLL)
    def _(step):
        base = pl.multiple_of(step * UNROLL, UNROLL)
        for k in range(UNROLL):
            above[pl.ds(base + k, 1), :] = ancestor[pl.ds(index_here[0, base + k], 1), :]

    get_couple.wait()
    rest = solved[...] - tall_product(couple_here[...], above[...])
    get_inv.wait()
    x_local[...] = wide_product(rest.T, inv_here[...])


def backward(one, root, solved, inv_local, couple_local, row_index, rows_one, rows_root, position):
    samples = solved.shape[1]
    x_local, own_one, own_root = pl.pallas_call(
        functools.partial(backward_kernel, position),
        out_shape=(
            jax.ShapeDtypeStruct(solved.shape[::-1], jnp.float32),
            jax.ShapeDtypeStruct((rows_one, samples), jnp.float32),
            jax.ShapeDtypeStruct((rows_root, samples), jnp.float32),
        ),
        in_specs=[VMEM, VMEM, VMEM, HBM, HBM, HBM],
        out_specs=(VMEM, VMEM, VMEM),
        scratch_shapes=[
            pltpu.VMEM(inv_local.shape, jnp.float32),
            pltpu.VMEM(couple_local.shape, jnp.float32),
            pltpu.SMEM(row_index.shape, row_index.dtype),
            pltpu.VMEM((2 * one.shape[0] * LANES, samples), jnp.float32),
            pltpu.VMEM((couple_local.shape[1], samples), jnp.float32),
            pltpu.SemaphoreType.DMA((3,)),
        ],
        compiler_params=pltpu.CompilerParams(vmem_limit_bytes=63 * 2**20),
        name="local_backward",
    )(one, root, solved, inv_local, couple_local, row_index)
    return x_local.T, own_one, own_root


def own_index():
    return own_position(EVERY)


def kernel_call(body, out_shapes, name):
    return pl.pallas_call(
        body,
        out_shape=tuple(jax.ShapeDtypeStruct(shape, jnp.float32) for shape in out_shapes),
        compiler_params=pltpu.CompilerParams(vmem_limit_bytes=16 * 2**20),
        name=name,
    )


def summed(parts):
    count = parts.shape[0]
    terms = [parts[k] for k in range(count)]
    while len(terms) > 1:
        terms = [a + b for a, b in zip(terms[::2], terms[1::2], strict=True)]
    return terms[0]


def pair_rows(stacked, rows, which):
    piece = stacked[:, rows + 8 * which : rows + 8 * which + 8, :]
    return piece.reshape(piece.shape[0] * 8, LANES)


def solve_one_kernel(parts, slots, out):
    samples = parts.shape[1]
    members = out.shape[0]
    right = summed(parts).T
    solved = [tall_product(pair_rows(slots, samples, g), right) for g in range(2)]
    blank = jnp.zeros((members * 8, LANES - 2 * samples), jnp.float32)
    out[...] = jnp.concatenate([*solved, blank], axis=1).reshape(members, 8, LANES)


def couple_up_kernel(parts, root, couple, out, solved):
    samples = root.shape[1]
    total_here = summed(parts)
    solved[...] = total_here
    flipped = total_here.T
    y = jnp.concatenate([flipped[:samples], flipped[samples : 2 * samples]], axis=1)
    lifted = wide_product(y, couple[...])
    for member in range(out.shape[0]):
        out[member] = root[member] - lifted[:, member * LANES : (member + 1) * LANES]


def solve_root_kernel(parts, slots, out):
    samples = parts.shape[1]
    members, rows, _ = out.shape
    first = slots.shape[1] - 8
    right = summed(parts).T
    y = tall_product(slots[:, first:, :].reshape(members * 8, LANES), right)
    y = jnp.concatenate([y[g * rows : (g + 1) * rows] for g in range(LANES // samples)], axis=1)
    for member in range(members):
        out[member] = y


def lift_root_kernel(parts, slots, out):
    members, rows, _ = parts.shape
    samples = out.shape[1]
    first = slots.shape[1] - 8
    flipped = summed(parts).T
    y = jnp.concatenate([flipped[g * samples : (g + 1) * samples] for g in range(LANES // samples)], axis=1)
    x = wide_product(y, slots[:, first:, :].reshape(members * 8, LANES))
    for member in range(out.shape[0]):
        out[member] = x


def rest_one_kernel(root, solved, couple, out):
    members, samples, _ = root.shape
    flat = jnp.concatenate([root[member] for member in range(members)], axis=1)
    flat = jnp.concatenate(halves(flat), axis=0)
    rows = couple.shape[0]
    both = jnp.concatenate(halves(couple[...]), axis=0)
    dims = (((1,), (1,)), ((), ()))
    every = lax.dot_general(both, flat, dims, preferred_element_type=jnp.float32)
    down = every[:rows, :samples] + (every[:rows, samples:] + every[rows:, :samples])
    blank = jnp.zeros((8, LANES - 2 * samples), jnp.float32)
    rest = solved[...] - jnp.concatenate([down[:8], down[8:], blank], axis=1)
    for member in range(members):
        out[member] = rest


def lift_one_kernel(parts, slots, out):
    members = parts.shape[0]
    samples = out.shape[1]
    flipped = parts[...].reshape(members * 8, LANES).T
    x = [wide_product(flipped[g * samples : (g + 1) * samples], pair_rows(slots, samples, g)) for g in range(2)]
    x = x[0] + x[1]
    for member in range(out.shape[0]):
        out[member] = x


def exchange(slots, axes):
    return lax.all_to_all(slots, axes, 0, 0)


def spread(value, axes):
    return exchange(jnp.broadcast_to(value[None], (lax.axis_size(axes),) + value.shape), axes)


def shards(
    rhs_local,
    inv_local,
    couple_local,
    row_index,
    rhs_sep1,
    inv_sep1,
    couple_sep1,
    rhs_sep0,
    inv_sep0,
):
    samples = rhs_local.shape[1]
    members = lax.axis_size(PLANE)
    piece = (samples, LANES)

    slots, root, solved_local = forward(
        rhs_local, inv_local, couple_local, row_index, rhs_sep1, inv_sep1, rhs_sep0, inv_sep0, own_index
    )
    slots = exchange(slots, PLANE)
    parts = spread(jnp.sum(slots[:, :samples], axis=0), HALF)
    (parts,) = kernel_call(solve_one_kernel, [(members, 8, LANES)], "solve_one")(parts, slots)
    parts, solved_one = kernel_call(couple_up_kernel, [(members, *piece), (8, LANES)], "couple_up")(
        exchange(parts, PLANE), root, couple_sep1
    )
    parts = spread(jnp.sum(exchange(parts, PLANE), axis=0), LINE)
    rows = members * rhs_sep0.shape[0] * samples // LANES
    (parts,) = kernel_call(solve_root_kernel, [(members, rows, LANES)], "solve_root")(parts, slots)
    (parts,) = kernel_call(lift_root_kernel, [(lax.axis_size(LINE), *piece)], "lift_root")(exchange(parts, PLANE), slots)
    x_root = spread(jnp.sum(exchange(parts, LINE), axis=0), PLANE)
    (parts,) = kernel_call(rest_one_kernel, [(members, 8, LANES)], "rest_one")(x_root, solved_one, couple_sep1)
    (parts,) = kernel_call(lift_one_kernel, [(lax.axis_size(HALF), *piece)], "lift_one")(exchange(parts, PLANE), slots)
    x_one = spread(jnp.sum(exchange(parts, HALF), axis=0), PLANE)
    return backward(
        x_one, x_root, solved_local, inv_local, couple_local, row_index, rhs_sep1.shape[0], rhs_sep0.shape[0], own_index
    )


def solution(mesh):
    leaf, blk = mesh.devices.shape
    halves_mesh = Mesh(mesh.devices.reshape(2, leaf // 4, 2, blk), EVERY)
    spec = P(EVERY, None)
    return jax.shard_map(shards, mesh=halves_mesh, in_specs=(spec,) * 9, out_specs=(spec,) * 3, check_vma=False)
```

time: 281 us -> 223 us (0.79)
  local copies, waits for them, and re-layouts: 31.5 us -> 0.15 us
  other arithmetic: 23.6 us -> 0.12 us
  matrix products: 17.8 us -> 0 us
  blocking collectives: 188 us -> 205 us
  Pallas kernels: 0 us -> 16.1 us
  waiting for transfers between devices: 11.2 us -> 0 us
  starting transfers between devices: 6.85 us -> 0 us
    dot_general x10 -> x0, matrix products: 17.8 us -> none  [product(): lax.dot_general(left, right, dims, precision=HIGHEST, preferred_element_t...]
    all_to_all x10 -> x11, blocking collectives: 188 us -> 205 us  [exchange(): return lax.all_to_all(slots, axes, 0, 0)]
    pallas_call x0 -> x8, Pallas kernels: none -> 16.1 us  [the longest x1 7.26 us: forward(): pl.pallas_call(functools.partial(forward_kernel, position), out_shape=(ja...]
    scatter-add x1 -> x0, other arithmetic: 11.3 us -> none  [shards(): jnp.zeros((2 * sep_rows, samples), jnp.float32).at[row_index[0]]]
    all_to_all x1 -> x0, waiting for transfers between devices: 11.2 us -> none  [exchange(): return lax.all_to_all(slots, axes, 0, 0)]
    unnamed x21 -> x6, local copies, waits for them, and re-layouts: 8.84 us -> 0.01 us
    all_to_all x1 -> x0, starting transfers between devices: 6.85 us -> none  [exchange(): return lax.all_to_all(slots, axes, 0, 0)]
    reduce_sum x8 -> x4, other arithmetic: 6.29 us -> 0.12 us  [the longest x1 0.05 us: shards(): parts = spread(jnp.sum(exchange(parts, PLANE), axis=0), LINE)]
  transfers between devices with their start and end apart: 1 -> 0, of which waited for: 1 -> 0; matrix products, arithmetic and copies ran while one was open for 0% -> 0% of each run, Pallas kernels for 0% -> 0%
where the time goes in v2:
time: 223 us; the launch traced here: 222 us
  blocking collectives  205 us (92%)
  Pallas kernels  16.1 us (7%)
    all_to_all x11, blocking collectives, exchange(): return lax.all_to_all(slots, axes, 0, 0)  205 us
    pallas_call x1, Pallas kernels, forward(): pl.pallas_call(functools.partial(forward_kernel, position), out_shape=(ja...  7.26 us
    pallas_call x1, Pallas kernels, backward(): pl.pallas_call(functools.partial(backward_kernel, position), out_shape=(j...  6.18 us

profile of v2, /device:TPU:1, one launch (start us, length us, event | category | flops | bytes accessed | tf_op | source)
XLA Modules:
  0.0 222.3 jit_solution(18214468662741467310)
XLA Ops:
  0.6 7.3 %local_forward.1 = (f32[32,56,128]{2,1,0:T(8,128)}, f32[32,32,128]{2,1,0:T(8,128)}, f32[512,32]{1,0:T(8,128)}) custom-call(f32[32,512]{1,0:T(8,128)} %bitcast.2, f32[512,512]{1,0:T(8,128)} %inv.3, f32[512,1536]{1,0:T(8,128)} %couple.7, s32[1,1536]{1,0:T(1,128)} %index.3, f32[16,32]{1,0:T(8,128)} %rhs_one.1, f32[16,4096]{1,0:T(8,128)} %inv_one.1, ...), custom_call_target="tpu_custom_call" | custom-call | tf_op jit(solution)/shard_map/local_forward/pallas_call | solution.py:142
  7.9 0.0 copy-start.1
  7.9 0.0 copy-start.2
  7.9 25.9 %all_to_all.55.slots = f32[32,56,128]{2,1,0:T(8,128)S(1)} all-to-all(f32[32,56,128]{2,1,0:T(8,128)} %get-tuple-element.11), channel_id=1, replica_groups=mesh['half'=2,'plane'=8,'core'=2,'blk'=16] {'core','blk'}, dimensions={0} | all-to-all | bytes 1835008 | tf_op jit(solution)/shard_map/all_to_all | solution.py:317
  33.9 20.3 %all_to_all.56.parts = f32[8,32,128]{2,1,0:T(8,128)S(1)} all-to-all(f32[8,32,128]{2,1,0:T(8,128)S(1)} %broadcast_in_dim.8), channel_id=1, replica_groups=mesh['half'=2,'plane'=8,'core'=2,'blk'=16] {'plane'}, dimensions={0} | all-to-all | bytes 262144 | tf_op jit(solution)/shard_map/all_to_all | solution.py:317
  54.2 0.5 solve_one.1
  54.8 13.8 %all_to_all.57.parts = f32[32,8,128]{2,1,0:T(8,128)S(1)} all-to-all(f32[32,8,128]{2,1,0:T(8,128)S(1)} %solve_one.1), channel_id=1, replica_groups=mesh['half'=2,'plane'=8,'core'=2,'blk'=16] {'core','blk'}, dimensions={0} | all-to-all | bytes 262144 | tf_op jit(solution)/shard_map/all_to_all | solution.py:317
  68.6 0.0 copy-done.1
  68.6 0.0 copy-done.2
  68.6 0.5 couple_up.1
  69.1 14.8 %all_to_all.58 = f32[32,32,128]{2,1,0:T(8,128)S(1)} all-to-all(f32[32,32,128]{2,1,0:T(8,128)S(1)} %get-tuple-element.13), channel_id=1, replica_groups=mesh['half'=2,'plane'=8,'core'=2,'blk'=16] {'core','blk'}, dimensions={0} | all-to-all | bytes 1048576 | tf_op jit(solution)/shard_map/all_to_all | solution.py:317
  83.9 20.1 %all_to_all.59.parts = f32[16,32,128]{2,1,0:T(8,128)S(1)} all-to-all(f32[16,32,128]{2,1,0:T(8,128)S(1)} %broadcast_in_dim.9), channel_id=1, replica_groups=mesh['half'=2,'plane'=8,'core'=2,'blk'=16] {'half','plane'}, dimensions={0} | all-to-all | bytes 524288 | tf_op jit(solution)/shard_map/all_to_all | solution.py:317
  104.0 0.6 solve_root.1
  104.6 26.5 %all_to_all.60.parts = f32[32,64,128]{2,1,0:T(8,128)S(1)} all-to-all(f32[32,64,128]{2,1,0:T(8,128)S(1)} %solve_root.1), channel_id=1, replica_groups=mesh['half'=2,'plane'=8,'core'=2,'blk'=16] {'core','blk'}, dimensions={0} | all-to-all | bytes 2097152 | tf_op jit(solution)/shard_map/all_to_all | solution.py:317
  131.1 0.4 lift_root.1
  131.5 18.2 %all_to_all.61 = f32[16,32,128]{2,1,0:T(8,128)S(1)} all-to-all(f32[16,32,128]{2,1,0:T(8,128)S(1)} %lift_root.1), channel_id=1, replica_groups=mesh['half'=2,'plane'=8,'core'=2,'blk'=16] {'half','plane'}, dimensions={0} | all-to-all | bytes 524288 | tf_op jit(solution)/shard_map/all_to_all | solution.py:317
  149.8 0.1 broadcast_in_dim.10
  149.8 21.2 %all_to_all.62.root = f32[32,32,128]{2,1,0:T(8,128)S(1)} all-to-all(f32[32,32,128]{2,1,0:T(8,128)S(1)} %broadcast_in_dim.10), channel_id=1, replica_groups=mesh['half'=2,'plane'=8,'core'=2,'blk'=16] {'core','blk'}, dimensions={0} | all-to-all | bytes 1048576 | tf_op jit(solution)/shard_map/all_to_all | solution.py:317
  171.0 0.0 copy-start
  171.0 0.5 rest_one.1
  171.5 11.5 %all_to_all.63.parts = f32[32,8,128]{2,1,0:T(8,128)S(1)} all-to-all(f32[32,8,128]{2,1,0:T(8,128)S(1)} %rest_one.1), channel_id=1, replica_groups=mesh['half'=2,'plane'=8,'core'=2,'blk'=16] {'core','blk'}, dimensions={0} | all-to-all | bytes 262144 | tf_op jit(solution)/shard_map/all_to_all | solution.py:317
  183.0 0.2 lift_one.1
  183.2 15.7 %all_to_all.64 = f32[8,32,128]{2,1,0:T(8,128)S(1)} all-to-all(f32[8,32,128]{2,1,0:T(8,128)S(1)} %lift_one.1), channel_id=1, replica_groups=mesh['half'=2,'plane'=8,'core'=2,'blk'=16] {'plane'}, dimensions={0} | all-to-all | bytes 262144 | tf_op jit(solution)/shard_map/all_to_all | solution.py:317
  198.9 0.1 broadcast_in_dim.11
  199.0 17.1 %all_to_all.65.one = f32[32,32,128]{2,1,0:T(8,128)} all-to-all(f32[32,32,128]{2,1,0:T(8,128)S(1)} %broadcast_in_dim.11), channel_id=1, replica_groups=mesh['half'=2,'plane'=8,'core'=2,'blk'=16] {'core','blk'}, dimensions={0} | all-to-all | bytes 1048576 | tf_op jit(solution)/shard_map/all_to_all | solution.py:317
  216.1 0.0 copy-done
  216.1 6.2 %local_backward.1 = (f32[32,512]{1,0:T(8,128)}, f32[16,32]{1,0:T(8,128)}, f32[8,32]{1,0:T(8,128)}) custom-call(f32[32,32,128]{2,1,0:T(8,128)} %all_to_all.65.one, f32[32,32,128]{2,1,0:T(8,128)} %copy-done, f32[512,32]{1,0:T(8,128)} %get-tuple-element.15.solved, f32[512,512]{1,0:T(8,128)} %inv.3, f32[512,1536]{1,0:T(8,128)} %couple.7, s32[1,1536]{1,0:T(1,128)} %index.3), custom_call_target="tpu_custom_call" | custom-call | tf_op jit(solution)/shard_map/local_backward/pallas_call | solution.py:200
  (6 shorter events, 0.2 us)
Async XLA Ops:
  7.9 60.7 %copy-start.1 = (f32[16,4096]{1,0:T(8,128)S(1)}, f32[16,4096]{1,0:T(8,128)}, u32[]{:S(2)}) copy-start(f32[16,4096]{1,0:T(8,128)} %couple.6) | copy-start | bytes 786436
  7.9 60.6 %copy-start.2 = (f32[32,32,128]{2,1,0:T(8,128)S(1)}, f32[32,32,128]{2,1,0:T(8,128)}, u32[]{:S(2)}) copy-start(f32[32,32,128]{2,1,0:T(8,128)} %get-tuple-element.12.root) | copy-start | bytes 1572868
  171.0 45.1 %copy-start = (f32[32,32,128]{2,1,0:T(8,128)}, f32[32,32,128]{2,1,0:T(8,128)S(1)}, u32[]{:S(2)}) copy-start(f32[32,32,128]{2,1,0:T(8,128)S(1)} %all_to_all.62.root) | copy-start | bytes 1572868

commit v3 on v2

v3 whole, which is shorter than its diff:
```python
import functools

import jax
import jax.numpy as jnp
from jax import lax
from jax.experimental import pallas as pl
from jax.experimental.pallas import tpu as pltpu
from jax.sharding import Mesh
from jax.sharding import PartitionSpec as P

GROUP = ("near", "core", "blk")
HALF = ("pair",)
LINE = ("half", "pair")
EVERY = LINE + GROUP

VMEM = pl.BlockSpec(memory_space=pltpu.VMEM)
SMEM = pl.BlockSpec(memory_space=pltpu.SMEM)
HBM = pl.BlockSpec(memory_space=pltpu.HBM)
LANES = 128
UNROLL = 32


def halves(value):
    high = value.astype(jnp.bfloat16)
    return high, (value - high.astype(jnp.float32)).astype(jnp.bfloat16)


def dot16(left, right):
    return jnp.dot(left, right, preferred_element_type=jnp.float32)


def tall_product(left, right):
    n = right.shape[1]
    left_high, left_low = halves(left)
    right_high, right_low = halves(right)
    both = dot16(left_high, jnp.concatenate([right_high, right_low], axis=1))
    return both[:, :n] + (both[:, n:] + dot16(left_low, right_high))


def wide_product(left, right):
    m = left.shape[0]
    left_high, left_low = halves(left)
    right_high, right_low = halves(right)
    both = dot16(jnp.concatenate([left_high, left_low], axis=0), right_high)
    return both[:m] + (both[m:] + dot16(left_high, right_low))


PILES = 4


def lane_piles(rows):
    return lax.broadcasted_iota(jnp.int32, (rows, LANES), 1) // (LANES // PILES)


def deal(stacks, width):
    granule = lax.broadcasted_iota(jnp.int32, stacks[0].shape, 1) // width
    turned = [stack if k == 0 else pltpu.roll(stack, width * k, 1) for k, stack in enumerate(stacks)]
    count = LANES // width
    for first in range(count):
        row = jnp.zeros_like(stacks[0])
        for k, stack in enumerate(turned):
            row = jnp.where(granule == (first + k) % count, stack, row)
        yield row if first == 0 else pltpu.roll(row, LANES - width * first, 1)


def fetch(pairs, sems):
    copies = [pltpu.make_async_copy(source, target, sems.at[k]) for k, (source, target) in enumerate(pairs)]
    for copy in copies:
        copy.start()
    return copies


def own_position(axes):
    position = lax.axis_index(axes[0])
    for axis in axes[1:]:
        position = position * lax.axis_size(axis) + lax.axis_index(axis)
    return position


def forward_kernel(
    position, rhs, inv, couple, index, rhs_one, inv_one, rhs_root, inv_root, slots, inv_slots, root, solved,
    rhs_here, inv_here, couple_here, index_here, rhs_one_here, inv_one_here, rhs_root_here, inv_root_here, update, lifted, sems,
):
    copies = fetch(
        [
            (inv_one, inv_one_here),
            (inv_root, inv_root_here),
            (rhs, rhs_here),
            (inv, inv_here),
            (index, index_here),
            (couple, couple_here),
            (rhs_one, rhs_one_here),
            (rhs_root, rhs_root_here),
        ],
        sems,
    )
    get_inv_one, get_inv_root, get_rhs, get_inv, get_index, get_couple, get_rhs_one, get_rhs_root = copies
    count = index.shape[1]
    rows_one = rhs_one.shape[0]
    rows_root = rhs_root.shape[0]
    sep_rows = inv_one.shape[1]
    pile = sep_rows // PILES
    depth = root.shape[1]

    @pl.loop(0, 2 * sep_rows // 512)
    def _(step):
        update[pl.ds(pl.multiple_of(step * 512, 512), 512), :] = jnp.zeros((512, LANES), jnp.float32)

    get_inv_one.wait()
    get_inv_root.wait()
    for first in range(0, pile, LANES):
        columns = [slice(g * pile + first, g * pile + first + LANES) for g in range(PILES)]
        stacks = [inv_one_here[r : r + rows_one // 2, c] for r in (0, rows_one // 2) for c in columns]
        for k, row in enumerate(deal(stacks, depth)):
            slots[first // depth + k, depth:, :] = row
        stacks = [inv_root_here[r : r + rows_root // 2, c] for r in (0, rows_root // 2) for c in columns]
        for k, row in enumerate(deal(stacks, depth)):
            inv_slots[first // depth + k, rows_root // 2 :, :] = row

    get_rhs.wait()
    get_inv.wait()
    y = tall_product(inv_here[...], rhs_here[...].T)
    solved[...] = y
    y = -y.T
    get_index.wait()
    get_couple.wait()
    step = couple_here.shape[1] // 2
    for start in range(0, couple_here.shape[1], step):
        part = wide_product(y, couple_here[:, start : start + step])
        lifted[start : start + step, :] = jnp.concatenate([part] * PILES, axis=0).T

    @pl.loop(0, count // UNROLL)
    def _(step):
        base = pl.multiple_of(step * UNROLL, UNROLL)
        for k in range(UNROLL):
            update[pl.ds(index_here[0, base + k], 1), :] = lifted[pl.ds(base + k, 1), :]

    get_rhs_one.wait()
    get_rhs_root.wait()
    here = position()
    own_one = pl.ds(pl.multiple_of(here % (sep_rows // rows_one) * rows_one, rows_one), rows_one)
    update[own_one, :] = update[own_one, :] + jnp.concatenate([rhs_one_here[...]] * PILES, axis=1)
    own_root = pl.ds(pl.multiple_of(sep_rows + here * rows_root, rows_root), rows_root)
    update[own_root, :] = update[own_root, :] + jnp.concatenate([rhs_root_here[...]] * PILES, axis=1)

    piles = lane_piles(depth)
    for base in (0, sep_rows):
        for member in range(root.shape[0]):
            rows = [update[base + g * pile + member * depth : base + g * pile + (member + 1) * depth, :] for g in range(PILES)]
            piece = rows[0]
            for g in range(1, PILES):
                piece = jnp.where(piles == g, rows[g], piece)
            if base == 0:
                slots[member, :depth, :] = piece
            else:
                root[member] = piece


def forward(rhs_local, inv_local, couple_local, row_index, rhs_sep1, inv_sep1, rhs_sep0, inv_sep0, position):
    samples = rhs_local.shape[1]
    members = lax.axis_size(GROUP)
    depth = inv_sep1.shape[1] // members // PILES
    slot_rows = depth + inv_sep1.shape[0] // 2
    given = (rhs_local.T, inv_local, couple_local, row_index, rhs_sep1, inv_sep1, rhs_sep0, inv_sep0)
    here = [pltpu.VMEM(array.shape, array.dtype) for array in given]
    here[3] = pltpu.SMEM(row_index.shape, row_index.dtype)
    return pl.pallas_call(
        functools.partial(forward_kernel, position),
        out_shape=(
            jax.ShapeDtypeStruct((members, slot_rows, LANES), jnp.float32),
            jax.ShapeDtypeStruct((members, inv_sep0.shape[0], LANES), jnp.float32),
            jax.ShapeDtypeStruct((members, depth, LANES), jnp.float32),
            jax.ShapeDtypeStruct(rhs_local.shape, jnp.float32),
        ),
        in_specs=[HBM] * len(given),
        out_specs=(VMEM, VMEM, VMEM, VMEM),
        scratch_shapes=here
        + [
            pltpu.VMEM((2 * inv_sep1.shape[1], LANES), jnp.float32),
            pltpu.VMEM((couple_local.shape[1], LANES), jnp.float32),
            pltpu.SemaphoreType.DMA((len(given),)),
        ],
        compiler_params=pltpu.CompilerParams(vmem_limit_bytes=63 * 2**20),
        name="local_forward",
    )(*given)


def backward_kernel(
    position, one, root, solved, inv, couple, index, x_local, own_one, own_root,
    inv_here, couple_here, index_here, ancestor, above, sems,
):
    get_index, get_couple, get_inv = fetch([(index, index_here), (couple, couple_here), (inv, inv_here)], sems)
    samples = solved.shape[1]
    count = index.shape[1]
    members, depth, _ = one.shape
    pile = members * depth
    sep_rows = PILES * pile
    piles = lane_piles(LANES)
    step = LANES // depth
    for base, source in ((0, one), (sep_rows, root)):
        for member in range(0, members, step):
            rows = source[member : member + step].reshape(LANES, LANES)
            for g in range(PILES):
                start = base + g * pile + member * depth
                ancestor[start : start + LANES, :] = jnp.where(piles == g, rows, 0.0)
    here = position()

    def take_own(start, out):
        wide = ancestor[pl.ds(pl.multiple_of(start, out.shape[0]), out.shape[0]), :]
        taken = wide[:, :samples]
        for g in range(1, PILES):
            taken = taken + wide[:, g * samples : (g + 1) * samples]
        out[...] = taken

    take_own(here % (sep_rows // own_one.shape[0]) * own_one.shape[0], own_one)
    take_own(sep_rows + here * own_root.shape[0], own_root)
    get_index.wait()

    @pl.loop(0, count // UNROLL)
    def _(step):
        base = pl.multiple_of(step * UNROLL, UNROLL)
        for k in range(UNROLL):
            above[pl.ds(base + k, 1), :] = ancestor[pl.ds(index_here[0, base + k], 1), :]

    get_couple.wait()
    down = tall_product(couple_here[...], above[...])
    rest = solved[...]
    for g in range(PILES):
        rest = rest - down[:, g * samples : (g + 1) * samples]
    get_inv.wait()
    x_local[...] = wide_product(rest.T, inv_here[...])


def backward(one, root, solved, inv_local, couple_local, row_index, rows_one, rows_root, position):
    samples = solved.shape[1]
    x_local, own_one, own_root = pl.pallas_call(
        functools.partial(backward_kernel, position),
        out_shape=(
            jax.ShapeDtypeStruct(solved.shape[::-1], jnp.float32),
            jax.ShapeDtypeStruct((rows_one, samples), jnp.float32),
            jax.ShapeDtypeStruct((rows_root, samples), jnp.float32),
        ),
        in_specs=[VMEM, VMEM, VMEM, HBM, HBM, HBM],
        out_specs=(VMEM, VMEM, VMEM),
        scratch_shapes=[
            pltpu.VMEM(inv_local.shape, jnp.float32),
            pltpu.VMEM(couple_local.shape, jnp.float32),
            pltpu.SMEM(row_index.shape, row_index.dtype),
            pltpu.VMEM((2 * PILES * one.shape[0] * one.shape[1], LANES), jnp.float32),
            pltpu.VMEM((couple_local.shape[1], LANES), jnp.float32),
            pltpu.SemaphoreType.DMA((3,)),
        ],
        compiler_params=pltpu.CompilerParams(vmem_limit_bytes=63 * 2**20),
        name="local_backward",
    )(one, root, solved, inv_local, couple_local, row_index)
    return x_local.T, own_one, own_root


def own_index():
    return own_position(EVERY)


def kernel_call(body, out_shapes, name, scratch=()):
    return pl.pallas_call(
        body,
        out_shape=tuple(jax.ShapeDtypeStruct(shape, jnp.float32) for shape in out_shapes),
        scratch_shapes=[pltpu.VMEM(shape, jnp.float32) for shape in scratch],
        compiler_params=pltpu.CompilerParams(vmem_limit_bytes=16 * 2**20),
        name=name,
    )


def summed(parts):
    terms = [parts[k] for k in range(parts.shape[0])]
    while len(terms) > 1:
        terms = [a + b for a, b in zip(terms[::2], terms[1::2], strict=True)]
    return terms[0]


def rows_of(piece):
    samples = LANES // PILES
    return jnp.concatenate([piece[:, g * samples : (g + 1) * samples] for g in range(PILES)], axis=0)


def piece_of(rows):
    depth = rows.shape[0] // PILES
    return jnp.concatenate([rows[g * depth : (g + 1) * depth] for g in range(PILES)], axis=1)


def inv_one_block(slots):
    piece = slots[:, slots.shape[1] - 8 :, :]
    return piece.reshape(piece.shape[0] * 8, LANES)


def inv_root_block(mixed):
    members = mixed.shape[0] // 8
    return jnp.concatenate([mixed[pl.ds(4 + i, members, stride=8), :] for i in range(4)], axis=0)


def twice(rows):
    blank = jnp.zeros_like(rows)
    return jnp.concatenate(
        [jnp.concatenate([rows, blank], axis=1), jnp.concatenate([blank, rows], axis=1)],
        axis=0,
    )


def solve_one_kernel(parts, slots, inv_slots, out, scratch):
    scratch[...] = tall_product(inv_one_block(slots), twice(rows_of(summed(parts))))
    members = scratch.shape[0] // 8
    out[...] = inv_slots[...]
    for i in range(4):
        pieces = [scratch[pl.ds(4 * h + i, members, stride=8), :] for h in range(2)]
        out[pl.ds(i, members, stride=8), :] = jnp.concatenate(pieces, axis=1)


def couple_up_kernel(parts, root, couple, out, solved):
    samples = LANES // PILES
    total_here = summed(parts)[: solved.shape[0]]
    solved[...] = total_here
    flipped = total_here.T
    order = [(g, h) for g in range(2) for h in range(2)]
    y = jnp.concatenate([flipped[(2 * h + g) * samples : (2 * h + g + 1) * samples] for g, h in order], axis=1)
    lifted = wide_product(y, couple[...])
    pile = lifted.shape[1] // PILES
    lifted = jnp.concatenate([lifted[:, g * pile : (g + 1) * pile] for g in range(PILES)], axis=0).T
    out[...] = root[...] - lifted.reshape(root.shape)


def solve_root_kernel(parts, mixed, out):
    y = tall_product(inv_root_block(mixed), twice(rows_of(summed(parts))))
    rows = out.shape[0]
    out[...] = jnp.concatenate([y[:rows], y[rows:]], axis=1)


def lift_root_kernel(solved, mixed, out):
    half = LANES // 2
    samples = LANES // PILES
    flipped = solved[...].T
    y = jnp.concatenate([flipped[:half], flipped[half:]], axis=1)
    every = wide_product(y, inv_root_block(mixed))
    piece = piece_of((every[:samples, :half] + every[samples:, half:]).T)
    for member in range(out.shape[0]):
        out[member] = piece


def rest_one_kernel(root, solved, couple, out):
    samples = LANES // PILES
    rows, columns = couple.shape
    pile = columns // PILES
    stacked = jnp.concatenate([couple[:, g * pile : (g + 1) * pile] for g in range(PILES)], axis=0)
    every = wide_product(stacked, root[...].reshape(pile, LANES))
    down = every[:rows, :samples]
    for g in range(1, PILES):
        down = down + every[g * rows : (g + 1) * rows, g * samples : (g + 1) * samples]
    order = [(h, g) for h in range(2) for g in range(2)]
    out[...] = solved[...] - jnp.concatenate([down[8 * g + 4 * h : 8 * g + 4 * h + 4] for h, g in order], axis=1)


def lift_one_kernel(rest, slots, out, scratch):
    samples = LANES // PILES
    members = rest.shape[0] // 4
    for i in range(4):
        pieces = rest[pl.ds(i, members, stride=4), :]
        for h in range(2):
            scratch[pl.ds(4 * h + i, members, stride=8), :] = pieces[:, 2 * samples * h : 2 * samples * (h + 1)]
    every = wide_product(scratch[...].T, inv_one_block(slots))
    half = LANES // 2
    piece = piece_of((every[:samples, :half] + every[samples:, half:]).T)
    for member in range(out.shape[0]):
        out[member] = piece


def exchange(slots, axes):
    return lax.all_to_all(slots, axes, 0, 0)


def spread(value, axes):
    return exchange(jnp.broadcast_to(value[None], (lax.axis_size(axes),) + value.shape), axes)


def shards(
    rhs_local,
    inv_local,
    couple_local,
    row_index,
    rhs_sep1,
    inv_sep1,
    couple_sep1,
    rhs_sep0,
    inv_sep0,
):
    samples = rhs_local.shape[1]
    members = lax.axis_size(GROUP)
    rows_one, rows_root = rhs_sep1.shape[0], rhs_sep0.shape[0]
    piece = (inv_sep0.shape[1] // members // PILES, LANES)
    block_one = (members * rows_one * samples // LANES, LANES)
    block_root = (members * rows_root * samples // LANES, LANES)
    flat_one = (members * rows_one // 2, 2 * samples)

    slots, inv_slots, root, solved_local = forward(
        rhs_local, inv_local, couple_local, row_index, rhs_sep1, inv_sep1, rhs_sep0, inv_sep0, own_index
    )
    slots = exchange(slots, GROUP)
    parts = spread(jnp.sum(slots[:, : piece[0]], axis=0), HALF)
    mixed = (members * inv_slots.shape[1], LANES)
    (parts,) = kernel_call(solve_one_kernel, [mixed], "solve_one", [flat_one])(parts, slots, inv_slots.reshape(mixed))
    parts = exchange(parts.reshape(members, -1, LANES), GROUP)
    mixed = parts.reshape(mixed)
    solved_shape = (block_one[0] // members, LANES)
    parts, solved_one = kernel_call(couple_up_kernel, [(members, *piece), solved_shape], "couple_up")(
        parts, root, couple_sep1
    )
    parts = spread(jnp.sum(exchange(parts, GROUP), axis=0), LINE)
    (parts,) = kernel_call(solve_root_kernel, [block_root], "solve_root")(parts, mixed)
    solved_root = jnp.sum(exchange(parts.reshape(members, -1, LANES), GROUP), axis=0)
    solved_root = spread(solved_root, GROUP).reshape(block_root)
    (parts,) = kernel_call(lift_root_kernel, [(lax.axis_size(LINE), *piece)], "lift_root")(solved_root, mixed)
    x_root = spread(jnp.sum(exchange(parts, LINE), axis=0), GROUP)
    (rest,) = kernel_call(rest_one_kernel, [solved_one.shape], "rest_one")(x_root, solved_one, couple_sep1)
    rest = spread(rest, GROUP).reshape(block_one)
    (parts,) = kernel_call(lift_one_kernel, [(lax.axis_size(HALF), *piece)], "lift_one", [flat_one])(rest, slots)
    x_one = spread(jnp.sum(exchange(parts, HALF), axis=0), GROUP)
    return backward(x_one, x_root, solved_local, inv_local, couple_local, row_index, rows_one, rows_root, own_index)


def solution(mesh):
    leaf, blk = mesh.devices.shape
    regrouped = Mesh(mesh.devices.reshape(2, leaf // 8, 2, 2, blk), EVERY)
    spec = P(EVERY, None)
    return jax.shard_map(shards, mesh=regrouped, in_specs=(spec,) * 9, out_specs=(spec,) * 3, check_vma=False)
```

time: 223 us -> 213 us (0.955)
  blocking collectives: 205 us -> 196 us
    all_to_all x11 -> x12, blocking collectives: 205 us -> 196 us  [exchange(): return lax.all_to_all(slots, axes, 0, 0)]
where the time goes in v3:
time: 213 us
  blocking collectives  196 us (92%)
  Pallas kernels  14.9 us (7%)
    all_to_all x12, blocking collectives, exchange(): return lax.all_to_all(slots, axes, 0, 0)  196 us
    pallas_call x1, Pallas kernels, forward(): pl.pallas_call(functools.partial(forward_kernel, position), out_shape=(ja...  6.2 us
    pallas_call x1, Pallas kernels, backward(): pl.pallas_call(functools.partial(backward_kernel, position), out_shape=(j...  5.6 us

profile of v3, /device:TPU:1, one launch (start us, length us, event | category | flops | bytes accessed | tf_op | source)
XLA Modules:
  0.0 212.8 jit_solution(7200734302554141372)
XLA Ops:
  0.6 6.2 %local_forward.1 = (f32[64,24,128]{2,1,0:T(8,128)}, f32[64,8,128]{2,1,0:T(8,128)}, f32[64,16,128]{2,1,0:T(8,128)}, f32[512,32]{1,0:T(8,128)}) custom-call(f32[32,512]{1,0:T(8,128)} %bitcast.15, f32[512,512]{1,0:T(8,128)} %inv.3, f32[512,1536]{1,0:T(8,128)} %couple.7, s32[1,1536]{1,0:T(1,128)} %index.3, f32[16,32]{1,0:T(8,128)} %rhs_one.1, ...), custom_call_target="tpu_custom_call" | custom-call | tf_op jit(solution)/shard_map/local_forward/pallas_call | solution.py:167
  6.8 0.0 copy-start.1
  6.8 0.0 copy-start.2
  6.9 25.2 %all_to_all.60.slots = f32[64,24,128]{2,1,0:T(8,128)S(1)} all-to-all(f32[64,24,128]{2,1,0:T(8,128)} %get-tuple-element.12), channel_id=1, replica_groups=mesh['half'=2,'pair'=4,'near'=2,'core'=2,'blk'=16] {'near','core','blk'}, dimensions={0} | all-to-all | bytes 1572864 | tf_op jit(solution)/shard_map/all_to_all | solution.py:375
  32.1 0.1 slice_reduce_fusion
  32.2 18.3 %all_to_all.61.parts = f32[4,16,128]{2,1,0:T(8,128)S(1)} all-to-all(f32[4,16,128]{2,1,0:T(8,128)S(1)} %broadcast_in_dim.12), channel_id=1, replica_groups=mesh['half'=2,'pair'=4,'near'=2,'core'=2,'blk'=16] {'pair'}, dimensions={0} | all-to-all | bytes 65536 | tf_op jit(solution)/shard_map/all_to_all | solution.py:375
  50.5 0.0 copy-start.3
  50.5 0.9 copy-done.3
  51.4 0.6 solve_one.1
  52.0 15.9 %all_to_all.62.parts = f32[64,8,128]{2,1,0:T(8,128)S(1)} all-to-all(f32[64,8,128]{2,1,0:T(8,128)S(1)} %bitcast.10), channel_id=1, replica_groups=mesh['half'=2,'pair'=4,'near'=2,'core'=2,'blk'=16] {'near','core','blk'}, dimensions={0} | all-to-all | bytes 524288 | tf_op jit(solution)/shard_map/all_to_all | solution.py:375
  68.0 0.0 copy-done.1
  68.0 0.0 copy-done.2
  68.0 0.7 couple_up.1
  68.7 16.2 %all_to_all.63 = f32[64,16,128]{2,1,0:T(8,128)S(1)} all-to-all(f32[64,16,128]{2,1,0:T(8,128)S(1)} %get-tuple-element.15), channel_id=1, replica_groups=mesh['half'=2,'pair'=4,'near'=2,'core'=2,'blk'=16] {'near','core','blk'}, dimensions={0} | all-to-all | bytes 1048576 | tf_op jit(solution)/shard_map/all_to_all | solution.py:375
  84.9 0.1 reduce_sum.46
  84.9 19.9 %all_to_all.64.parts = f32[8,16,128]{2,1,0:T(8,128)S(1)} all-to-all(f32[8,16,128]{2,1,0:T(8,128)S(1)} %broadcast_in_dim.13), channel_id=1, replica_groups=mesh['half'=2,'pair'=4,'near'=2,'core'=2,'blk'=16] {'half','pair'}, dimensions={0} | all-to-all | bytes 131072 | tf_op jit(solution)/shard_map/all_to_all | solution.py:375
  104.8 0.5 solve_root.1
  105.4 14.4 %all_to_all.65 = f32[64,2,128]{2,1,0:T(2,128)S(1)} all-to-all(f32[64,2,128]{2,1,0:T(2,128)S(1)} %bitcast.13), channel_id=1, replica_groups=mesh['half'=2,'pair'=4,'near'=2,'core'=2,'blk'=16] {'near','core','blk'}, dimensions={0} | all-to-all | bytes 131072 | tf_op jit(solution)/shard_map/all_to_all | solution.py:375
  119.8 0.1 reduce_sum.47
  119.9 12.2 %all_to_all.66 = f32[64,2,128]{2,1,0:T(2,128)S(1)} all-to-all(f32[64,2,128]{2,1,0:T(2,128)S(1)} %broadcast_in_dim.14), channel_id=1, replica_groups=mesh['half'=2,'pair'=4,'near'=2,'core'=2,'blk'=16] {'near','core','blk'}, dimensions={0} | all-to-all | bytes 131072 | tf_op jit(solution)/shard_map/all_to_all | solution.py:375
  132.1 0.4 lift_root.1
  132.6 14.4 %all_to_all.67 = f32[8,16,128]{2,1,0:T(8,128)S(1)} all-to-all(f32[8,16,128]{2,1,0:T(8,128)S(1)} %lift_root.1), channel_id=1, replica_groups=mesh['half'=2,'pair'=4,'near'=2,'core'=2,'blk'=16] {'half','pair'}, dimensions={0} | all-to-all | bytes 131072 | tf_op jit(solution)/shard_map/all_to_all | solution.py:375
  147.1 17.6 %all_to_all.68.root = f32[64,16,128]{2,1,0:T(8,128)S(1)} all-to-all(f32[64,16,128]{2,1,0:T(8,128)S(1)} %broadcast_in_dim.15), channel_id=1, replica_groups=mesh['half'=2,'pair'=4,'near'=2,'core'=2,'blk'=16] {'near','core','blk'}, dimensions={0} | all-to-all | bytes 1048576 | tf_op jit(solution)/shard_map/all_to_all | solution.py:375
  164.7 0.0 copy-start
  164.7 0.4 rest_one.1
  165.1 13.4 %all_to_all.69 = f32[64,4,128]{2,1,0:T(4,128)S(1)} all-to-all(f32[64,4,128]{2,1,0:T(4,128)S(1)} %broadcast_in_dim.16), channel_id=1, replica_groups=mesh['half'=2,'pair'=4,'near'=2,'core'=2,'blk'=16] {'near','core','blk'}, dimensions={0} | all-to-all | bytes 262144 | tf_op jit(solution)/shard_map/all_to_all | solution.py:375
  178.5 0.5 lift_one.1
  179.0 10.8 %all_to_all.70 = f32[4,16,128]{2,1,0:T(8,128)S(1)} all-to-all(f32[4,16,128]{2,1,0:T(8,128)S(1)} %lift_one.1), channel_id=1, replica_groups=mesh['half'=2,'pair'=4,'near'=2,'core'=2,'blk'=16] {'pair'}, dimensions={0} | all-to-all | bytes 65536 | tf_op jit(solution)/shard_map/all_to_all | solution.py:375
  189.9 17.3 %all_to_all.71.one = f32[64,16,128]{2,1,0:T(8,128)} all-to-all(f32[64,16,128]{2,1,0:T(8,128)S(1)} %broadcast_in_dim.17), channel_id=1, replica_groups=mesh['half'=2,'pair'=4,'near'=2,'core'=2,'blk'=16] {'near','core','blk'}, dimensions={0} | all-to-all | bytes 1048576 | tf_op jit(solution)/shard_map/all_to_all | solution.py:375
  207.2 0.0 copy-done
  207.2 5.6 %local_backward.1 = (f32[32,512]{1,0:T(8,128)}, f32[16,32]{1,0:T(8,128)}, f32[8,32]{1,0:T(8,128)}) custom-call(f32[64,16,128]{2,1,0:T(8,128)} %all_to_all.71.one, f32[64,16,128]{2,1,0:T(8,128)} %copy-done, f32[512,32]{1,0:T(8,128)} %get-tuple-element.17.solved, f32[512,512]{1,0:T(8,128)} %inv.3, f32[512,1536]{1,0:T(8,128)} %couple.7, s32[1,1536]{1,0:T(1,128)} %index.3), custom_call_target="tpu_custom_call" | custom-call | tf_op jit(solution)/shard_map/local_backward/pallas_call | solution.py:236
  (8 shorter events, 0.1 us)
Async XLA Ops:
  6.8 61.1 %copy-start.1 = (f32[16,4096]{1,0:T(8,128)S(1)}, f32[16,4096]{1,0:T(8,128)}, u32[]{:S(2)}) copy-start(f32[16,4096]{1,0:T(8,128)} %couple.6) | copy-start | bytes 786436
  6.8 61.1 %copy-start.2 = (f32[64,16,128]{2,1,0:T(8,128)S(1)}, f32[64,16,128]{2,1,0:T(8,128)}, u32[]{:S(2)}) copy-start(f32[64,16,128]{2,1,0:T(8,128)} %get-tuple-element.14.root) | copy-start | bytes 1572868
  50.5 1.0 copy-start.3
  164.7 42.5 %copy-start = (f32[64,16,128]{2,1,0:T(8,128)}, f32[64,16,128]{2,1,0:T(8,128)S(1)}, u32[]{:S(2)}) copy-start(f32[64,16,128]{2,1,0:T(8,128)S(1)} %all_to_all.68.root) | copy-start | bytes 1572868

commit v4 on v3

--- a/solution.py
+++ b/solution.py
@@ -78,82 +78,114 @@
 
 
 def forward_kernel(
-    position, rhs, inv, couple, index, rhs_one, inv_one, rhs_root, inv_root, slots, inv_slots, root, solved,
-    rhs_here, inv_here, couple_here, index_here, rhs_one_here, inv_one_here, rhs_root_here, inv_root_here, update, lifted, sems,
+    position, rhs, inv, couple, index, rhs_one, inv_one, slots, solved, lifted_out,
+    rhs_here, inv_here, couple_here, index_here, index_wide, rhs_one_here, inv_one_here, update, lifted, sems,
 ):
+    quarter = couple.shape[1] // 4
+    quarters = [slice(k * quarter, (k + 1) * quarter) for k in range(4)]
     copies = fetch(
         [
+            (rhs, rhs_here),
             (inv_one, inv_one_here),
-            (inv_root, inv_root_here),
-            (rhs, rhs_here),
             (inv, inv_here),
             (index, index_here),
-            (couple, couple_here),
+            (index, index_wide),
+            *[(couple.at[:, columns], couple_here.at[:, columns]) for columns in quarters],
             (rhs_one, rhs_one_here),
-            (rhs_root, rhs_root_here),
         ],
         sems,
     )
-    get_inv_one, get_inv_root, get_rhs, get_inv, get_index, get_couple, get_rhs_one, get_rhs_root = copies
-    count = index.shape[1]
+    get_rhs, get_inv_one, get_inv, get_index, get_index_wide, *get_couple, get_rhs_one = copies
+    samples = rhs.shape[0]
     rows_one = rhs_one.shape[0]
-    rows_root = rhs_root.shape[0]
     sep_rows = inv_one.shape[1]
     pile = sep_rows // PILES
-    depth = root.shape[1]
-
-    @pl.loop(0, 2 * sep_rows // 512)
-    def _(step):
-        update[pl.ds(pl.multiple_of(step * 512, 512), 512), :] = jnp.zeros((512, LANES), jnp.float32)
-
+    depth = slots.shape[1] - rows_one // 2
+    clear(update, 0, sep_rows)
+
+    get_rhs.wait()
     get_inv_one.wait()
-    get_inv_root.wait()
     for first in range(0, pile, LANES):
         columns = [slice(g * pile + first, g * pile + first + LANES) for g in range(PILES)]
         stacks = [inv_one_here[r : r + rows_one // 2, c] for r in (0, rows_one // 2) for c in columns]
         for k, row in enumerate(deal(stacks, depth)):
             slots[first // depth + k, depth:, :] = row
-        stacks = [inv_root_here[r : r + rows_root // 2, c] for r in (0, rows_root // 2) for c in columns]
-        for k, row in enumerate(deal(stacks, depth)):
-            inv_slots[first // depth + k, rows_root // 2 :, :] = row
-
-    get_rhs.wait()
+
     get_inv.wait()
     y = tall_product(inv_here[...], rhs_here[...].T)
     solved[...] = y
     y = -y.T
     get_index.wait()
-    get_couple.wait()
-    step = couple_here.shape[1] // 2
-    for start in range(0, couple_here.shape[1], step):
-        part = wide_product(y, couple_here[:, start : start + step])
-        lifted[start : start + step, :] = jnp.concatenate([part] * PILES, axis=0).T
-
-    @pl.loop(0, count // UNROLL)
+    get_index_wide.wait()
+    low = jnp.sum((index_wide[...] < sep_rows).astype(jnp.int32))
+    for copy, columns in zip(get_couple, quarters, strict=True):
+        copy.wait()
+        part = wide_product(y, couple_here[:, columns])
+        lifted_out[:, columns] = part
+        lifted[columns, :] = jnp.concatenate([part] * PILES, axis=0).T
+
+    scatter_rows(update, lifted, index_here, 0, (low + UNROLL - 1) // UNROLL)
+
+    get_rhs_one.wait()
+    own_one = pl.ds(pl.multiple_of(position() % (sep_rows // rows_one) * rows_one, rows_one), rows_one)
+    update[own_one, :] = update[own_one, :] + jnp.concatenate([rhs_one_here[...]] * PILES, axis=1)
+    for member in range(slots.shape[0]):
+        slots[member, :depth, :] = merged(update, 0, member, depth, pile)
+
+
+def clear(target, start, rows):
+    @pl.loop(0, rows // 512)
+    def _(step):
+        target[pl.ds(pl.multiple_of(start + step * 512, 512), 512), :] = jnp.zeros((512, LANES), jnp.float32)
+
+
+def scatter_rows(target, source, index, first, last):
+    @pl.loop(first, last)
     def _(step):
         base = pl.multiple_of(step * UNROLL, UNROLL)
         for k in range(UNROLL):
-            update[pl.ds(index_here[0, base + k], 1), :] = lifted[pl.ds(base + k, 1), :]
-
-    get_rhs_one.wait()
-    get_rhs_root.wait()
-    here = position()
-    own_one = pl.ds(pl.multiple_of(here % (sep_rows // rows_one) * rows_one, rows_one), rows_one)
-    update[own_one, :] = update[own_one, :] + jnp.concatenate([rhs_one_here[...]] * PILES, axis=1)
-    own_root = pl.ds(pl.multiple_of(sep_rows + here * rows_root, rows_root), rows_root)
+            target[pl.ds(index[0, base + k], 1), :] = source[pl.ds(base + k, 1), :]
+
+
+def merged(update, base, member, depth, pile):
+    starts = [base + g * pile + member * depth for g in range(PILES)]
+    piles = lane_piles(depth)
+    piece = update[starts[0] : starts[0] + depth, :]
+    for g in range(1, PILES):
+        piece = jnp.where(piles == g, update[starts[g] : starts[g] + depth, :], piece)
+    return piece
+
+
+def root_kernel(
+    position, lifted_wide, index, rhs_root, inv_root, inv_slots, root,
+    index_here, index_wide, rhs_root_here, inv_root_here, update, lifted, sems,
+):
+    copies = fetch(
+        [(index, index_here), (index, index_wide), (rhs_root, rhs_root_here), (inv_root, inv_root_here)], sems
+    )
+    rows_root = rhs_root.shape[0]
+    sep_rows = inv_root.shape[1]
+    pile = sep_rows // PILES
+    depth = root.shape[1]
+    clear(update, sep_rows, sep_rows)
+    lifted[...] = jnp.concatenate([lifted_wide[...]] * PILES, axis=0).T
+    for copy in copies:
+        copy.wait()
+    low = jnp.sum((index_wide[...] < sep_rows).astype(jnp.int32))
+    scatter_rows(update, lifted, index_here, low // UNROLL, index.shape[1] // UNROLL)
+    own_root = pl.ds(pl.multiple_of(sep_rows + position() * rows_root, rows_root), rows_root)
     update[own_root, :] = update[own_root, :] + jnp.concatenate([rhs_root_here[...]] * PILES, axis=1)
-
-    piles = lane_piles(depth)
-    for base in (0, sep_rows):
-        for member in range(root.shape[0]):
-            rows = [update[base + g * pile + member * depth : base + g * pile + (member + 1) * depth, :] for g in range(PILES)]
-            piece = rows[0]
-            for g in range(1, PILES):
-                piece = jnp.where(piles == g, rows[g], piece)
-            if base == 0:
-                slots[member, :depth, :] = piece
-            else:
-                root[member] = piece
+    for member in range(root.shape[0]):
+        root[member] = merged(update, sep_rows, member, depth, pile)
+    for first in range(0, pile, LANES):
+        columns = [slice(g * pile + first, g * pile + first + LANES) for g in range(PILES)]
+        stacks = [inv_root_here[r : r + rows_root // 2, c] for r in (0, rows_root // 2) for c in columns]
+        for k, row in enumerate(deal(stacks, depth)):
+            inv_slots[first // depth + k, rows_root // 2 :, :] = row
+
+
+def like(array):
+    return pltpu.VMEM(array.shape, array.dtype)
 
 
 def forward(rhs_local, inv_local, couple_local, row_index, rhs_sep1, inv_sep1, rhs_sep0, inv_sep0, position):
@@ -161,72 +193,116 @@
     members = lax.axis_size(GROUP)
     depth = inv_sep1.shape[1] // members // PILES
     slot_rows = depth + inv_sep1.shape[0] // 2
-    given = (rhs_local.T, inv_local, couple_local, row_index, rhs_sep1, inv_sep1, rhs_sep0, inv_sep0)
-    here = [pltpu.VMEM(array.shape, array.dtype) for array in given]
-    here[3] = pltpu.SMEM(row_index.shape, row_index.dtype)
-    return pl.pallas_call(
+    given = (rhs_local.T, inv_local, couple_local, row_index, rhs_sep1, inv_sep1)
+    wide = pltpu.VMEM((couple_local.shape[1], LANES), jnp.float32)
+    update = pltpu.VMEM((2 * inv_sep1.shape[1], LANES), jnp.float32)
+    index_here = pltpu.SMEM(row_index.shape, row_index.dtype)
+    slots, solved, lifted = pl.pallas_call(
         functools.partial(forward_kernel, position),
         out_shape=(
             jax.ShapeDtypeStruct((members, slot_rows, LANES), jnp.float32),
-            jax.ShapeDtypeStruct((members, inv_sep0.shape[0], LANES), jnp.float32),
-            jax.ShapeDtypeStruct((members, depth, LANES), jnp.float32),
             jax.ShapeDtypeStruct(rhs_local.shape, jnp.float32),
+            jax.ShapeDtypeStruct((samples, couple_local.shape[1]), jnp.float32),
         ),
         in_specs=[HBM] * len(given),
-        out_specs=(VMEM, VMEM, VMEM, VMEM),
-        scratch_shapes=here
-        + [
-            pltpu.VMEM((2 * inv_sep1.shape[1], LANES), jnp.float32),
-            pltpu.VMEM((couple_local.shape[1], LANES), jnp.float32),
-            pltpu.SemaphoreType.DMA((len(given),)),
+        out_specs=(VMEM, VMEM, VMEM),
+        scratch_shapes=[
+            *[like(array) for array in given[:3]],
+            index_here,
+            like(row_index),
+            like(rhs_sep1),
+            like(inv_sep1),
+            update,
+            wide,
+            pltpu.SemaphoreType.DMA((10,)),
         ],
         compiler_params=pltpu.CompilerParams(vmem_limit_bytes=63 * 2**20),
         name="local_forward",
     )(*given)
-
-
-def backward_kernel(
-    position, one, root, solved, inv, couple, index, x_local, own_one, own_root,
-    inv_here, couple_here, index_here, ancestor, above, sems,
-):
-    get_index, get_couple, get_inv = fetch([(index, index_here), (couple, couple_here), (inv, inv_here)], sems)
-    samples = solved.shape[1]
-    count = index.shape[1]
-    members, depth, _ = one.shape
-    pile = members * depth
-    sep_rows = PILES * pile
+    inv_slots, root = pl.pallas_call(
+        functools.partial(root_kernel, position),
+        out_shape=(
+            jax.ShapeDtypeStruct((members, inv_sep0.shape[0], LANES), jnp.float32),
+            jax.ShapeDtypeStruct((members, depth, LANES), jnp.float32),
+        ),
+        in_specs=[VMEM, HBM, HBM, HBM],
+        out_specs=(VMEM, VMEM),
+        scratch_shapes=[
+            index_here,
+            like(row_index),
+            like(rhs_sep0),
+            like(inv_sep0),
+            update,
+            wide,
+            pltpu.SemaphoreType.DMA((4,)),
+        ],
+        compiler_params=pltpu.CompilerParams(vmem_limit_bytes=24 * 2**20),
+        name="local_root",
+    )(lifted, row_index, rhs_sep0, inv_sep0)
+    return slots, inv_slots, root, solved
+
+
+def spread_rows(target, base, source):
+    members, depth, _ = source.shape
     piles = lane_piles(LANES)
     step = LANES // depth
-    for base, source in ((0, one), (sep_rows, root)):
-        for member in range(0, members, step):
-            rows = source[member : member + step].reshape(LANES, LANES)
-            for g in range(PILES):
-                start = base + g * pile + member * depth
-                ancestor[start : start + LANES, :] = jnp.where(piles == g, rows, 0.0)
-    here = position()
-
-    def take_own(start, out):
-        wide = ancestor[pl.ds(pl.multiple_of(start, out.shape[0]), out.shape[0]), :]
-        taken = wide[:, :samples]
-        for g in range(1, PILES):
-            taken = taken + wide[:, g * samples : (g + 1) * samples]
-        out[...] = taken
-
-    take_own(here % (sep_rows // own_one.shape[0]) * own_one.shape[0], own_one)
-    take_own(sep_rows + here * own_root.shape[0], own_root)
-    get_index.wait()
-
-    @pl.loop(0, count // UNROLL)
+    for member in range(0, members, step):
+        rows = source[member : member + step].reshape(LANES, LANES)
+        for g in range(PILES):
+            start = base + (g * members + member) * depth
+            target[start : start + LANES, :] = jnp.where(piles == g, rows, 0.0)
+
+
+def folded(wide):
+    samples = LANES // PILES
+    total_here = wide[:, :samples]
+    for g in range(1, PILES):
+        total_here = total_here + wide[:, g * samples : (g + 1) * samples]
+    return total_here
+
+
+def own_rows(table, start, rows):
+    return folded(table[pl.ds(pl.multiple_of(start, rows), rows), :])
+
+
+def gather_rows(target, source, index, first, last):
+    @pl.loop(first, last)
     def _(step):
         base = pl.multiple_of(step * UNROLL, UNROLL)
         for k in range(UNROLL):
-            above[pl.ds(base + k, 1), :] = ancestor[pl.ds(index_here[0, base + k], 1), :]
-
+            target[pl.ds(base + k, 1), :] = source[pl.ds(index[0, base + k], 1), :]
+
+
+def backward_kernel(
+    position, one, root, solved, inv, couple, index, x_local, own_one, own_root,
+    one_here, root_here, solved_here, inv_here, couple_here, index_here, ancestor, above, sems,
+):
+    get_one, get_root, get_index, get_couple, get_solved, get_inv = fetch(
+        [
+            (one, one_here),
+            (root, root_here),
+            (index, index_here),
+            (couple, couple_here),
+            (solved, solved_here),
+            (inv, inv_here),
+        ],
+        sems,
+    )
+    sep_rows = PILES * one.shape[0] * one.shape[1]
+    rows_one = own_one.shape[0]
+    rows_root = own_root.shape[0]
+    get_one.wait()
+    spread_rows(ancestor, 0, one_here)
+    get_root.wait()
+    spread_rows(ancestor, sep_rows, root_here)
+    here = position()
+    own_one[...] = own_rows(ancestor, here % (sep_rows // rows_one) * rows_one, rows_one)
+    own_root[...] = own_rows(ancestor, sep_rows + here * rows_root, rows_root)
+    get_index.wait()
+    gather_rows(above, ancestor, index_here, 0, index.shape[1] // UNROLL)
     get_couple.wait()
-    down = tall_product(couple_here[...], above[...])
-    rest = solved[...]
-    for g in range(PILES):
-        rest = rest - down[:, g * samples : (g + 1) * samples]
+    get_solved.wait()
+    rest = solved_here[...] - folded(tall_product(couple_here[...], above[...]))
     get_inv.wait()
     x_local[...] = wide_product(rest.T, inv_here[...])
 
@@ -240,15 +316,18 @@
             jax.ShapeDtypeStruct((rows_one, samples), jnp.float32),
             jax.ShapeDtypeStruct((rows_root, samples), jnp.float32),
         ),
-        in_specs=[VMEM, VMEM, VMEM, HBM, HBM, HBM],
+        in_specs=[HBM] * 6,
         out_specs=(VMEM, VMEM, VMEM),
         scratch_shapes=[
-            pltpu.VMEM(inv_local.shape, jnp.float32),
-            pltpu.VMEM(couple_local.shape, jnp.float32),
+            like(one),
+            like(root),
+            like(solved),
+            like(inv_local),
+            like(couple_local),
             pltpu.SMEM(row_index.shape, row_index.dtype),
             pltpu.VMEM((2 * PILES * one.shape[0] * one.shape[1], LANES), jnp.float32),
             pltpu.VMEM((couple_local.shape[1], LANES), jnp.float32),
-            pltpu.SemaphoreType.DMA((3,)),
+            pltpu.SemaphoreType.DMA((6,)),
         ],
         compiler_params=pltpu.CompilerParams(vmem_limit_bytes=63 * 2**20),
         name="local_backward",
@@ -401,7 +480,7 @@
     slots, inv_slots, root, solved_local = forward(
         rhs_local, inv_local, couple_local, row_index, rhs_sep1, inv_sep1, rhs_sep0, inv_sep0, own_index
     )
-    slots = exchange(slots, GROUP)
+    slots, inv_slots, root = lax.optimization_barrier((exchange(slots, GROUP), inv_slots, root))
     parts = spread(jnp.sum(slots[:, : piece[0]], axis=0), HALF)
     mixed = (members * inv_slots.shape[1], LANES)
     (parts,) = kernel_call(solve_one_kernel, [mixed], "solve_one", [flat_one])(parts, slots, inv_slots.reshape(mixed))

time: 213 us -> 212 us (level)
  blocking collectives: 196 us -> 171 us
  starting transfers between devices: 0 us -> 11.2 us
  waiting for transfers between devices: 0 us -> 11.1 us
    all_to_all x12 -> x11, blocking collectives: 196 us -> 171 us  [exchange(): return lax.all_to_all(slots, axes, 0, 0)]
    all_to_all x0 -> x1, starting transfers between devices: none -> 11.2 us  [exchange(): return lax.all_to_all(slots, axes, 0, 0)]
    all_to_all x0 -> x1, waiting for transfers between devices: none -> 11.1 us  [exchange(): return lax.all_to_all(slots, axes, 0, 0)]
  transfers between devices with their start and end apart: 0 -> 1, of which waited for: 0 -> 1; matrix products, arithmetic and copies ran while one was open for 0% -> 0% of each run, Pallas kernels for 0% -> 1%
where the time goes in v4:
time: 212 us; the launch traced here: 211 us
  blocking collectives  171 us (81%)
  Pallas kernels  15.7 us (7%)
  starting transfers between devices  11.2 us (5%)
  waiting for transfers between devices  11.1 us (5%)
    all_to_all x11, blocking collectives, exchange(): return lax.all_to_all(slots, axes, 0, 0)  171 us
    all_to_all x1, starting transfers between devices, exchange(): return lax.all_to_all(slots, axes, 0, 0)  11.2 us
    all_to_all x1, waiting for transfers between devices, exchange(): return lax.all_to_all(slots, axes, 0, 0)  11.1 us
    pallas_call x1, Pallas kernels, forward(): pl.pallas_call(functools.partial(forward_kernel, position), out_shape=(ja...  5.75 us
    pallas_call x1, Pallas kernels, backward(): pl.pallas_call(functools.partial(backward_kernel, position), out_shape=(j...  4.98 us
  transfers between devices with their start and end apart: 1, of which 1 were waited for; matrix products, arithmetic and copies ran while one was open for 0% of the time, Pallas kernels for 1%

profile of v4, /device:TPU:1, one launch (start us, length us, event | category | flops | bytes accessed | tf_op | source)
XLA Modules:
  0.0 211.2 jit_solution(12655862466938929996)
XLA Ops:
  0.6 0.0 copy-start.4
  0.6 0.0 copy-start.3
  0.7 0.0 copy-start.5
  0.7 5.8 %local_forward.1 = (f32[64,24,128]{2,1,0:T(8,128)}, f32[512,32]{1,0:T(8,128)}, f32[32,1536]{1,0:T(8,128)}) custom-call(f32[32,512]{1,0:T(8,128)} %bitcast.15, f32[512,512]{1,0:T(8,128)} %inv.3, f32[512,1536]{1,0:T(8,128)} %couple.7, s32[1,1536]{1,0:T(1,128)} %index.5, f32[16,32]{1,0:T(8,128)} %rhs_one.1, f32[16,4096]{1,0:T(8,128)} %inv_one.1), custom_call_target="tpu_custom_call" | custom-call | tf_op jit(solution)/shard_map/local_forward/pallas_call | solution.py:200
  6.4 0.0 copy-start.1
  6.4 11.2 %all-to-all-start = ((f32[64,24,128]{2,1,0:T(8,128)}), f32[64,24,128]{2,1,0:T(8,128)S(1)}, u32[]{:S(2)}, u32[]{:S(2)}) async-start(f32[64,24,128]{2,1,0:T(8,128)} %get-tuple-element.16), calls=%async_computation | async-start | bytes 1572864 | tf_op jit(solution)/shard_map/all_to_all | solution.py:454
  17.6 0.0 copy-done.4
  17.7 0.9 copy-done.2
  18.6 1.9 local_root.1
  20.5 11.1 %all-to-all-done.slots = f32[64,24,128]{2,1,0:T(8,128)S(1)} async-done(((f32[64,24,128]{2,1,0:T(8,128)}), f32[64,24,128]{2,1,0:T(8,128)S(1)}, u32[]{:S(2)}, u32[]{:S(2)}) %all-to-all-start) | async-done | bytes 786464 | tf_op jit(solution)/shard_map/all_to_all | solution.py:454
  31.6 0.1 slice_reduce_fusion
  31.7 18.4 %all_to_all.60.parts = f32[4,16,128]{2,1,0:T(8,128)S(1)} all-to-all(f32[4,16,128]{2,1,0:T(8,128)S(1)} %broadcast_in_dim.12), channel_id=1, replica_groups=mesh['half'=2,'pair'=4,'near'=2,'core'=2,'blk'=16] {'pair'}, dimensions={0} | all-to-all | bytes 65536 | tf_op jit(solution)/shard_map/all_to_all | solution.py:454
  50.0 0.6 solve_one.1
  50.6 15.9 %all_to_all.61.parts = f32[64,8,128]{2,1,0:T(8,128)S(1)} all-to-all(f32[64,8,128]{2,1,0:T(8,128)S(1)} %bitcast.10), channel_id=1, replica_groups=mesh['half'=2,'pair'=4,'near'=2,'core'=2,'blk'=16] {'near','core','blk'}, dimensions={0} | all-to-all | bytes 524288 | tf_op jit(solution)/shard_map/all_to_all | solution.py:454
  66.6 0.7 couple_up.1
  67.3 16.2 %all_to_all.62 = f32[64,16,128]{2,1,0:T(8,128)S(1)} all-to-all(f32[64,16,128]{2,1,0:T(8,128)S(1)} %get-tuple-element.23), channel_id=1, replica_groups=mesh['half'=2,'pair'=4,'near'=2,'core'=2,'blk'=16] {'near','core','blk'}, dimensions={0} | all-to-all | bytes 1048576 | tf_op jit(solution)/shard_map/all_to_all | solution.py:454
  83.5 0.1 reduce_sum.46
  83.5 20.0 %all_to_all.63.parts = f32[8,16,128]{2,1,0:T(8,128)S(1)} all-to-all(f32[8,16,128]{2,1,0:T(8,128)S(1)} %broadcast_in_dim.13), channel_id=1, replica_groups=mesh['half'=2,'pair'=4,'near'=2,'core'=2,'blk'=16] {'half','pair'}, dimensions={0} | all-to-all | bytes 131072 | tf_op jit(solution)/shard_map/all_to_all | solution.py:454
  103.5 0.5 solve_root.1
  104.0 14.4 %all_to_all.64 = f32[64,2,128]{2,1,0:T(2,128)S(1)} all-to-all(f32[64,2,128]{2,1,0:T(2,128)S(1)} %bitcast.13), channel_id=1, replica_groups=mesh['half'=2,'pair'=4,'near'=2,'core'=2,'blk'=16] {'near','core','blk'}, dimensions={0} | all-to-all | bytes 131072 | tf_op jit(solution)/shard_map/all_to_all | solution.py:454
  118.4 0.1 reduce_sum.47
  118.5 12.2 %all_to_all.65 = f32[64,2,128]{2,1,0:T(2,128)S(1)} all-to-all(f32[64,2,128]{2,1,0:T(2,128)S(1)} %broadcast_in_dim.14), channel_id=1, replica_groups=mesh['half'=2,'pair'=4,'near'=2,'core'=2,'blk'=16] {'near','core','blk'}, dimensions={0} | all-to-all | bytes 131072 | tf_op jit(solution)/shard_map/all_to_all | solution.py:454
  130.8 0.4 lift_root.1
  131.2 14.4 %all_to_all.66 = f32[8,16,128]{2,1,0:T(8,128)S(1)} all-to-all(f32[8,16,128]{2,1,0:T(8,128)S(1)} %lift_root.1), channel_id=1, replica_groups=mesh['half'=2,'pair'=4,'near'=2,'core'=2,'blk'=16] {'half','pair'}, dimensions={0} | all-to-all | bytes 131072 | tf_op jit(solution)/shard_map/all_to_all | solution.py:454
  145.7 17.6 %all_to_all.67.root = f32[64,16,128]{2,1,0:T(8,128)S(1)} all-to-all(f32[64,16,128]{2,1,0:T(8,128)S(1)} %broadcast_in_dim.15), channel_id=1, replica_groups=mesh['half'=2,'pair'=4,'near'=2,'core'=2,'blk'=16] {'near','core','blk'}, dimensions={0} | all-to-all | bytes 1048576 | tf_op jit(solution)/shard_map/all_to_all | solution.py:454
  163.3 0.4 rest_one.1
  163.8 13.4 %all_to_all.68 = f32[64,4,128]{2,1,0:T(4,128)S(1)} all-to-all(f32[64,4,128]{2,1,0:T(4,128)S(1)} %broadcast_in_dim.16), channel_id=1, replica_groups=mesh['half'=2,'pair'=4,'near'=2,'core'=2,'blk'=16] {'near','core','blk'}, dimensions={0} | all-to-all | bytes 262144 | tf_op jit(solution)/shard_map/all_to_all | solution.py:454
  177.2 0.5 lift_one.1
  177.7 10.8 %all_to_all.69 = f32[4,16,128]{2,1,0:T(8,128)S(1)} all-to-all(f32[4,16,128]{2,1,0:T(8,128)S(1)} %lift_one.1), channel_id=1, replica_groups=mesh['half'=2,'pair'=4,'near'=2,'core'=2,'blk'=16] {'pair'}, dimensions={0} | all-to-all | bytes 65536 | tf_op jit(solution)/shard_map/all_to_all | solution.py:454
  188.5 17.5 %all_to_all.70.one = f32[64,16,128]{2,1,0:T(8,128)} all-to-all(f32[64,16,128]{2,1,0:T(8,128)S(1)} %broadcast_in_dim.17), channel_id=1, replica_groups=mesh['half'=2,'pair'=4,'near'=2,'core'=2,'blk'=16] {'near','core','blk'}, dimensions={0} | all-to-all | bytes 1048576 | tf_op jit(solution)/shard_map/all_to_all | solution.py:454
  206.0 0.0 copy-done
  206.0 5.0 %local_backward.1 = (f32[32,512]{1,0:T(8,128)}, f32[16,32]{1,0:T(8,128)}, f32[8,32]{1,0:T(8,128)}) custom-call(f32[64,16,128]{2,1,0:T(8,128)} %all_to_all.70.one, f32[64,16,128]{2,1,0:T(8,128)} %copy-done, f32[512,32]{1,0:T(8,128)} %get-tuple-element.25.solved, f32[512,512]{1,0:T(8,128)} %inv.3, f32[512,1536]{1,0:T(8,128)} %couple.7, s32[1,1536]{1,0:T(1,128)} %index.5), custom_call_target="tpu_custom_call" | custom-call | tf_op jit(solution)/shard_map/local_backward/pallas_call | solution.py:312
  (13 shorter events, 0.2 us)
Async XLA Ops:
  0.6 17.0 %copy-start.4 = (s32[1,1536]{1,0:T(1,128)S(1)}, s32[1,1536]{1,0:T(1,128)}, u32[]{:S(2)}) copy-start(s32[1,1536]{1,0:T(1,128)} %index.5) | copy-start | bytes 18436
  0.6 17.0 %copy-start.3 = (f32[8,4096]{1,0:T(8,128)S(1)}, f32[8,4096]{1,0:T(8,128)}, u32[]{:S(2)}) copy-start(f32[8,4096]{1,0:T(8,128)} %inv_root.1) | copy-start | bytes 393220
  0.7 17.0 %copy-start.5 = (f32[8,32]{1,0:T(8,128)S(1)}, f32[8,32]{1,0:T(8,128)}, u32[]{:S(2)}) copy-start(f32[8,32]{1,0:T(8,128)} %rhs_root.1) | copy-start | bytes 3076
  6.4 60.1 %copy-start.1 = (f32[16,4096]{1,0:T(8,128)S(1)}, f32[16,4096]{1,0:T(8,128)}, u32[]{:S(2)}) copy-start(f32[16,4096]{1,0:T(8,128)} %couple.6) | copy-start | bytes 786436
  6.4 25.2 %all-to-all-start = ((f32[64,24,128]{2,1,0:T(8,128)}), f32[64,24,128]{2,1,0:T(8,128)S(1)}, u32[]{:S(2)}, u32[]{:S(2)}) async-start(f32[64,24,128]{2,1,0:T(8,128)} %get-tuple-element.16), calls=%async_computation | async-start | bytes 1572864 | tf_op jit(solution)/shard_map/all_to_all | solution.py:454
  17.7 0.9 copy-start.2
  163.3 42.7 %copy-start = (f32[64,16,128]{2,1,0:T(8,128)}, f32[64,16,128]{2,1,0:T(8,128)S(1)}, u32[]{:S(2)}) copy-start(f32[64,16,128]{2,1,0:T(8,128)S(1)} %all_to_all.67.root) | copy-start | bytes 1572868

commit v5 on v4

--- a/solution.py
+++ b/solution.py
@@ -79,23 +79,24 @@
 
 def forward_kernel(
     position, rhs, inv, couple, index, rhs_one, inv_one, slots, solved, lifted_out,
-    rhs_here, inv_here, couple_here, index_here, index_wide, rhs_one_here, inv_one_here, update, lifted, sems,
+    rhs_here, inv_here, couple_here, index_here, index_wide, rhs_one_here, inv_one_here, update, lifted,
+    slots_here, solved_here, lifted_here, sems, out_sems,
 ):
     quarter = couple.shape[1] // 4
     quarters = [slice(k * quarter, (k + 1) * quarter) for k in range(4)]
     copies = fetch(
         [
-            (rhs, rhs_here),
-            (inv_one, inv_one_here),
-            (inv, inv_here),
             (index, index_here),
             (index, index_wide),
+            (inv_one, inv_one_here),
+            (rhs, rhs_here),
+            (inv, inv_here),
             *[(couple.at[:, columns], couple_here.at[:, columns]) for columns in quarters],
             (rhs_one, rhs_one_here),
         ],
         sems,
     )
-    get_rhs, get_inv_one, get_inv, get_index, get_index_wide, *get_couple, get_rhs_one = copies
+    get_index, get_index_wide, get_inv_one, get_rhs, get_inv, *get_couple, get_rhs_one = copies
     samples = rhs.shape[0]
     rows_one = rhs_one.shape[0]
     sep_rows = inv_one.shape[1]
@@ -103,34 +104,44 @@
     depth = slots.shape[1] - rows_one // 2
     clear(update, 0, sep_rows)
 
-    get_rhs.wait()
+    get_index.wait()
+    get_index_wide.wait()
+    low = jnp.sum((index_wide[...] < sep_rows).astype(jnp.int32))
     get_inv_one.wait()
     for first in range(0, pile, LANES):
         columns = [slice(g * pile + first, g * pile + first + LANES) for g in range(PILES)]
         stacks = [inv_one_here[r : r + rows_one // 2, c] for r in (0, rows_one // 2) for c in columns]
         for k, row in enumerate(deal(stacks, depth)):
-            slots[first // depth + k, depth:, :] = row
-
+            slots_here[first // depth + k, depth:, :] = row
+    puts = fetch([(slots_here.at[:, depth:, :], slots.at[:, depth:, :])], out_sems.at[:1])
+
+    get_rhs.wait()
     get_inv.wait()
-    y = tall_product(inv_here[...], rhs_here[...].T)
-    solved[...] = y
-    y = -y.T
-    get_index.wait()
-    get_index_wide.wait()
-    low = jnp.sum((index_wide[...] < sep_rows).astype(jnp.int32))
+    y = tall_product(inv_here[...], rhs_here[...].T).T
+    solved_here[...] = y
+    puts += fetch([(solved_here, solved)], out_sems.at[1:2])
+    y = -y
     for copy, columns in zip(get_couple, quarters, strict=True):
         copy.wait()
         part = wide_product(y, couple_here[:, columns])
-        lifted_out[:, columns] = part
+        lifted_here[:, columns] = part
         lifted[columns, :] = jnp.concatenate([part] * PILES, axis=0).T
+
+    puts += fetch([(lifted_here, lifted_out)], out_sems.at[2:3])
 
     scatter_rows(update, lifted, index_here, 0, (low + UNROLL - 1) // UNROLL)
 
     get_rhs_one.wait()
     own_one = pl.ds(pl.multiple_of(position() % (sep_rows // rows_one) * rows_one, rows_one), rows_one)
     update[own_one, :] = update[own_one, :] + jnp.concatenate([rhs_one_here[...]] * PILES, axis=1)
-    for member in range(slots.shape[0]):
-        slots[member, :depth, :] = merged(update, 0, member, depth, pile)
+    members = slots.shape[0]
+    for k in range(2):
+        some = slice(k * members // 2, (k + 1) * members // 2)
+        for member in range(some.start, some.stop):
+            slots_here[member, :depth, :] = merged(update, 0, member, depth, pile)
+        puts += fetch([(slots_here.at[some, :depth, :], slots.at[some, :depth, :])], out_sems.at[3 + k : 4 + k])
+    for put in puts:
+        put.wait()
 
 
 def clear(target, start, rows):
@@ -201,11 +212,11 @@
         functools.partial(forward_kernel, position),
         out_shape=(
             jax.ShapeDtypeStruct((members, slot_rows, LANES), jnp.float32),
-            jax.ShapeDtypeStruct(rhs_local.shape, jnp.float32),
+            jax.ShapeDtypeStruct(rhs_local.shape[::-1], jnp.float32),
             jax.ShapeDtypeStruct((samples, couple_local.shape[1]), jnp.float32),
         ),
         in_specs=[HBM] * len(given),
-        out_specs=(VMEM, VMEM, VMEM),
+        out_specs=(HBM, HBM, HBM),
         scratch_shapes=[
             *[like(array) for array in given[:3]],
             index_here,
@@ -214,7 +225,11 @@
             like(inv_sep1),
             update,
             wide,
+            pltpu.VMEM((members, slot_rows, LANES), jnp.float32),
+            pltpu.VMEM(rhs_local.shape[::-1], jnp.float32),
+            pltpu.VMEM((samples, couple_local.shape[1]), jnp.float32),
             pltpu.SemaphoreType.DMA((10,)),
+            pltpu.SemaphoreType.DMA((5,)),
         ],
         compiler_params=pltpu.CompilerParams(vmem_limit_bytes=63 * 2**20),
         name="local_forward",
@@ -302,17 +317,17 @@
     gather_rows(above, ancestor, index_here, 0, index.shape[1] // UNROLL)
     get_couple.wait()
     get_solved.wait()
-    rest = solved_here[...] - folded(tall_product(couple_here[...], above[...]))
+    rest = solved_here[...] - folded(tall_product(couple_here[...], above[...])).T
     get_inv.wait()
-    x_local[...] = wide_product(rest.T, inv_here[...])
+    x_local[...] = wide_product(rest, inv_here[...])
 
 
 def backward(one, root, solved, inv_local, couple_local, row_index, rows_one, rows_root, position):
-    samples = solved.shape[1]
+    samples = solved.shape[0]
     x_local, own_one, own_root = pl.pallas_call(
         functools.partial(backward_kernel, position),
         out_shape=(
-            jax.ShapeDtypeStruct(solved.shape[::-1], jnp.float32),
+            jax.ShapeDtypeStruct(solved.shape, jnp.float32),
             jax.ShapeDtypeStruct((rows_one, samples), jnp.float32),
             jax.ShapeDtypeStruct((rows_root, samples), jnp.float32),
         ),
@@ -400,10 +415,14 @@
     flipped = total_here.T
     order = [(g, h) for g in range(2) for h in range(2)]
     y = jnp.concatenate([flipped[(2 * h + g) * samples : (2 * h + g + 1) * samples] for g, h in order], axis=1)
-    lifted = wide_product(y, couple[...])
-    pile = lifted.shape[1] // PILES
-    lifted = jnp.concatenate([lifted[:, g * pile : (g + 1) * pile] for g in range(PILES)], axis=0).T
-    out[...] = root[...] - lifted.reshape(root.shape)
+    pile = couple.shape[1] // PILES
+    members = LANES // root.shape[1]
+    for first in range(0, pile, LANES):
+        columns = [slice(g * pile + first, g * pile + first + LANES) for g in range(PILES)]
+        lifted = wide_product(y, jnp.concatenate([couple[:, c] for c in columns], axis=1))
+        lifted = jnp.concatenate([lifted[:, g * LANES : (g + 1) * LANES] for g in range(PILES)], axis=0).T
+        some = slice(first // LANES * members, (first // LANES + 1) * members)
+        out[some] = root[some] - lifted.reshape(members, *root.shape[1:])
 
 
 def solve_root_kernel(parts, mixed, out):

time: 212 us -> 212 us (level)
  no operation moved by 1% of the time
where the time goes in v5:
time: 212 us; the launch traced here: 211 us
  blocking collectives  171 us (81%)
  Pallas kernels  15.5 us (7%)
  starting transfers between devices  11.2 us (5%)
  waiting for transfers between devices  11.1 us (5%)
    all_to_all x11, blocking collectives, exchange(): return lax.all_to_all(slots, axes, 0, 0)  171 us
    all_to_all x1, starting transfers between devices, exchange(): return lax.all_to_all(slots, axes, 0, 0)  11.2 us
    all_to_all x1, waiting for transfers between devices, exchange(): return lax.all_to_all(slots, axes, 0, 0)  11.1 us
    pallas_call x1, Pallas kernels, forward(): pl.pallas_call(functools.partial(forward_kernel, position), out_shape=(ja...  5.55 us
    pallas_call x1, Pallas kernels, backward(): pl.pallas_call(functools.partial(backward_kernel, position), out_shape=(j...  5.06 us
  transfers between devices with their start and end apart: 1, of which 1 were waited for; matrix products, arithmetic and copies ran while one was open for 0% of the time, Pallas kernels for 1%

profile of v5, /device:TPU:1, one launch (start us, length us, event | category | flops | bytes accessed | tf_op | source)
XLA Modules:
  0.0 211.0 jit_solution(4932788079322166131)
XLA Ops:
  0.6 0.0 copy-start.4
  0.6 0.0 copy-start.3
  0.7 0.0 copy-start.5
  0.7 5.6 %local_forward.1 = (f32[64,24,128]{2,1,0:T(8,128)}, f32[32,512]{1,0:T(8,128)}, f32[32,1536]{1,0:T(8,128)}) custom-call(f32[32,512]{1,0:T(8,128)} %bitcast.15, f32[512,512]{1,0:T(8,128)} %inv.3, f32[512,1536]{1,0:T(8,128)} %couple.7, s32[1,1536]{1,0:T(1,128)} %index.5, f32[16,32]{1,0:T(8,128)} %rhs_one.1, f32[16,4096]{1,0:T(8,128)} %inv_one.1), custom_call_target="tpu_custom_call" | custom-call | tf_op jit(solution)/shard_map/local_forward/pallas_call | solution.py:211
  6.2 0.0 copy-start.1
  6.2 11.2 %all-to-all-start = ((f32[64,24,128]{2,1,0:T(8,128)}), f32[64,24,128]{2,1,0:T(8,128)S(1)}, u32[]{:S(2)}, u32[]{:S(2)}) async-start(f32[64,24,128]{2,1,0:T(8,128)} %get-tuple-element.16), calls=%async_computation | async-start | bytes 1572864 | tf_op jit(solution)/shard_map/all_to_all | solution.py:473
  17.4 0.0 copy-done.4
  17.5 0.9 copy-done.2
  18.4 1.9 local_root.1
  20.3 11.1 %all-to-all-done.slots = f32[64,24,128]{2,1,0:T(8,128)S(1)} async-done(((f32[64,24,128]{2,1,0:T(8,128)}), f32[64,24,128]{2,1,0:T(8,128)S(1)}, u32[]{:S(2)}, u32[]{:S(2)}) %all-to-all-start) | async-done | bytes 786464 | tf_op jit(solution)/shard_map/all_to_all | solution.py:473
  31.4 0.1 slice_reduce_fusion
  31.5 18.4 %all_to_all.60.parts = f32[4,16,128]{2,1,0:T(8,128)S(1)} all-to-all(f32[4,16,128]{2,1,0:T(8,128)S(1)} %broadcast_in_dim.12), channel_id=1, replica_groups=mesh['half'=2,'pair'=4,'near'=2,'core'=2,'blk'=16] {'pair'}, dimensions={0} | all-to-all | bytes 65536 | tf_op jit(solution)/shard_map/all_to_all | solution.py:473
  49.9 0.6 solve_one.1
  50.4 15.9 %all_to_all.61.parts = f32[64,8,128]{2,1,0:T(8,128)S(1)} all-to-all(f32[64,8,128]{2,1,0:T(8,128)S(1)} %bitcast.10), channel_id=1, replica_groups=mesh['half'=2,'pair'=4,'near'=2,'core'=2,'blk'=16] {'near','core','blk'}, dimensions={0} | all-to-all | bytes 524288 | tf_op jit(solution)/shard_map/all_to_all | solution.py:473
  66.4 0.6 couple_up.1
  67.0 16.2 %all_to_all.62 = f32[64,16,128]{2,1,0:T(8,128)S(1)} all-to-all(f32[64,16,128]{2,1,0:T(8,128)S(1)} %get-tuple-element.23), channel_id=1, replica_groups=mesh['half'=2,'pair'=4,'near'=2,'core'=2,'blk'=16] {'near','core','blk'}, dimensions={0} | all-to-all | bytes 1048576 | tf_op jit(solution)/shard_map/all_to_all | solution.py:473
  83.2 0.1 reduce_sum.46
  83.3 19.9 %all_to_all.63.parts = f32[8,16,128]{2,1,0:T(8,128)S(1)} all-to-all(f32[8,16,128]{2,1,0:T(8,128)S(1)} %broadcast_in_dim.13), channel_id=1, replica_groups=mesh['half'=2,'pair'=4,'near'=2,'core'=2,'blk'=16] {'half','pair'}, dimensions={0} | all-to-all | bytes 131072 | tf_op jit(solution)/shard_map/all_to_all | solution.py:473
  103.2 0.5 solve_root.1
  103.7 14.4 %all_to_all.64 = f32[64,2,128]{2,1,0:T(2,128)S(1)} all-to-all(f32[64,2,128]{2,1,0:T(2,128)S(1)} %bitcast.13), channel_id=1, replica_groups=mesh['half'=2,'pair'=4,'near'=2,'core'=2,'blk'=16] {'near','core','blk'}, dimensions={0} | all-to-all | bytes 131072 | tf_op jit(solution)/shard_map/all_to_all | solution.py:473
  118.1 0.1 reduce_sum.47
  118.2 12.2 %all_to_all.65 = f32[64,2,128]{2,1,0:T(2,128)S(1)} all-to-all(f32[64,2,128]{2,1,0:T(2,128)S(1)} %broadcast_in_dim.14), channel_id=1, replica_groups=mesh['half'=2,'pair'=4,'near'=2,'core'=2,'blk'=16] {'near','core','blk'}, dimensions={0} | all-to-all | bytes 131072 | tf_op jit(solution)/shard_map/all_to_all | solution.py:473
  130.5 0.4 lift_root.1
  130.9 14.4 %all_to_all.66 = f32[8,16,128]{2,1,0:T(8,128)S(1)} all-to-all(f32[8,16,128]{2,1,0:T(8,128)S(1)} %lift_root.1), channel_id=1, replica_groups=mesh['half'=2,'pair'=4,'near'=2,'core'=2,'blk'=16] {'half','pair'}, dimensions={0} | all-to-all | bytes 131072 | tf_op jit(solution)/shard_map/all_to_all | solution.py:473
  145.4 17.6 %all_to_all.67.root = f32[64,16,128]{2,1,0:T(8,128)S(1)} all-to-all(f32[64,16,128]{2,1,0:T(8,128)S(1)} %broadcast_in_dim.15), channel_id=1, replica_groups=mesh['half'=2,'pair'=4,'near'=2,'core'=2,'blk'=16] {'near','core','blk'}, dimensions={0} | all-to-all | bytes 1048576 | tf_op jit(solution)/shard_map/all_to_all | solution.py:473
  163.0 0.4 rest_one.1
  163.5 13.4 %all_to_all.68 = f32[64,4,128]{2,1,0:T(4,128)S(1)} all-to-all(f32[64,4,128]{2,1,0:T(4,128)S(1)} %broadcast_in_dim.16), channel_id=1, replica_groups=mesh['half'=2,'pair'=4,'near'=2,'core'=2,'blk'=16] {'near','core','blk'}, dimensions={0} | all-to-all | bytes 262144 | tf_op jit(solution)/shard_map/all_to_all | solution.py:473
  176.8 0.5 lift_one.1
  177.4 10.8 %all_to_all.69 = f32[4,16,128]{2,1,0:T(8,128)S(1)} all-to-all(f32[4,16,128]{2,1,0:T(8,128)S(1)} %lift_one.1), channel_id=1, replica_groups=mesh['half'=2,'pair'=4,'near'=2,'core'=2,'blk'=16] {'pair'}, dimensions={0} | all-to-all | bytes 65536 | tf_op jit(solution)/shard_map/all_to_all | solution.py:473
  188.2 17.5 %all_to_all.70.one = f32[64,16,128]{2,1,0:T(8,128)} all-to-all(f32[64,16,128]{2,1,0:T(8,128)S(1)} %broadcast_in_dim.17), channel_id=1, replica_groups=mesh['half'=2,'pair'=4,'near'=2,'core'=2,'blk'=16] {'near','core','blk'}, dimensions={0} | all-to-all | bytes 1048576 | tf_op jit(solution)/shard_map/all_to_all | solution.py:473
  205.7 0.0 copy-done
  205.7 5.1 %local_backward.1 = (f32[32,512]{1,0:T(8,128)}, f32[16,32]{1,0:T(8,128)}, f32[8,32]{1,0:T(8,128)}) custom-call(f32[64,16,128]{2,1,0:T(8,128)} %all_to_all.70.one, f32[64,16,128]{2,1,0:T(8,128)} %copy-done, f32[32,512]{1,0:T(8,128)} %get-tuple-element.25.solved, f32[512,512]{1,0:T(8,128)} %inv.3, f32[512,1536]{1,0:T(8,128)} %couple.7, s32[1,1536]{1,0:T(1,128)} %index.5), custom_call_target="tpu_custom_call" | custom-call | tf_op jit(solution)/shard_map/local_backward/pallas_call | solution.py:327
  (13 shorter events, 0.2 us)
Async XLA Ops:
  0.6 16.8 %copy-start.4 = (s32[1,1536]{1,0:T(1,128)S(1)}, s32[1,1536]{1,0:T(1,128)}, u32[]{:S(2)}) copy-start(s32[1,1536]{1,0:T(1,128)} %index.5) | copy-start | bytes 18436
  0.6 16.8 %copy-start.3 = (f32[8,4096]{1,0:T(8,128)S(1)}, f32[8,4096]{1,0:T(8,128)}, u32[]{:S(2)}) copy-start(f32[8,4096]{1,0:T(8,128)} %inv_root.1) | copy-start | bytes 393220
  0.7 16.8 %copy-start.5 = (f32[8,32]{1,0:T(8,128)S(1)}, f32[8,32]{1,0:T(8,128)}, u32[]{:S(2)}) copy-start(f32[8,32]{1,0:T(8,128)} %rhs_root.1) | copy-start | bytes 3076
  6.2 60.2 %copy-start.1 = (f32[16,4096]{1,0:T(8,128)S(1)}, f32[16,4096]{1,0:T(8,128)}, u32[]{:S(2)}) copy-start(f32[16,4096]{1,0:T(8,128)} %couple.6) | copy-start | bytes 786436
  6.2 25.2 %all-to-all-start = ((f32[64,24,128]{2,1,0:T(8,128)}), f32[64,24,128]{2,1,0:T(8,128)S(1)}, u32[]{:S(2)}, u32[]{:S(2)}) async-start(f32[64,24,128]{2,1,0:T(8,128)} %get-tuple-element.16), calls=%async_computation | async-start | bytes 1572864 | tf_op jit(solution)/shard_map/all_to_all | solution.py:473
  17.5 0.9 copy-start.2
  163.0 42.7 %copy-start = (f32[64,16,128]{2,1,0:T(8,128)}, f32[64,16,128]{2,1,0:T(8,128)S(1)}, u32[]{:S(2)}) copy-start(f32[64,16,128]{2,1,0:T(8,128)S(1)} %all_to_all.67.root) | copy-start | bytes 1572868

commit v6 on v5

--- a/solution.py
+++ b/solution.py
@@ -18,6 +18,7 @@
 HBM = pl.BlockSpec(memory_space=pltpu.HBM)
 LANES = 128
 UNROLL = 32
+WIDE = 128
 
 
 def halves(value):
@@ -283,8 +284,8 @@
 def gather_rows(target, source, index, first, last):
     @pl.loop(first, last)
     def _(step):
-        base = pl.multiple_of(step * UNROLL, UNROLL)
-        for k in range(UNROLL):
+        base = pl.multiple_of(step * WIDE, WIDE)
+        for k in range(WIDE):
             target[pl.ds(base + k, 1), :] = source[pl.ds(index[0, base + k], 1), :]
 
 
@@ -314,10 +315,18 @@
     own_one[...] = own_rows(ancestor, here % (sep_rows // rows_one) * rows_one, rows_one)
     own_root[...] = own_rows(ancestor, sep_rows + here * rows_root, rows_root)
     get_index.wait()
-    gather_rows(above, ancestor, index_here, 0, index.shape[1] // UNROLL)
+    gather_rows(above, ancestor, index_here, 0, index.shape[1] // WIDE)
     get_couple.wait()
     get_solved.wait()
-    rest = solved_here[...] - folded(tall_product(couple_here[...], above[...])).T
+    held = halves(above[...])
+    both = jnp.concatenate(held, axis=1)
+    rows = couple_here.shape[0] // 4
+    downs = []
+    for k in range(4):
+        high, low = halves(couple_here[k * rows : (k + 1) * rows, :])
+        part = dot16(high, both)
+        downs.append(folded(part[:, :LANES] + (part[:, LANES:] + dot16(low, held[0]))).T)
+    rest = solved_here[...] - jnp.concatenate(downs, axis=1)
     get_inv.wait()
     x_local[...] = wide_product(rest, inv_here[...])
 

time: 212 us -> 211 us (level)
  no operation moved by 1% of the time
where the time goes in v6:
time: 211 us
  blocking collectives  171 us (81%)
  Pallas kernels  15.3 us (7%)
  starting transfers between devices  11.2 us (5%)
  waiting for transfers between devices  11.1 us (5%)
    all_to_all x11, blocking collectives, exchange(): return lax.all_to_all(slots, axes, 0, 0)  171 us
    all_to_all x1, starting transfers between devices, exchange(): return lax.all_to_all(slots, axes, 0, 0)  11.2 us
    all_to_all x1, waiting for transfers between devices, exchange(): return lax.all_to_all(slots, axes, 0, 0)  11.1 us
    pallas_call x1, Pallas kernels, forward(): pl.pallas_call(functools.partial(forward_kernel, position), out_shape=(ja...  5.55 us
    pallas_call x1, Pallas kernels, backward(): pl.pallas_call(functools.partial(backward_kernel, position), out_shape=(j...  4.83 us
  transfers between devices with their start and end apart: 1, of which 1 were waited for; matrix products, arithmetic and copies ran while one was open for 0% of the time, Pallas kernels for 1%

profile of v6, /device:TPU:1, one launch (start us, length us, event | category | flops | bytes accessed | tf_op | source)
XLA Modules:
  0.0 210.8 jit_solution(17562409269736797183)
XLA Ops:
  0.6 0.0 copy-start.4
  0.6 0.0 copy-start.3
  0.7 0.0 copy-start.5
  0.7 5.6 %local_forward.1 = (f32[64,24,128]{2,1,0:T(8,128)}, f32[32,512]{1,0:T(8,128)}, f32[32,1536]{1,0:T(8,128)}) custom-call(f32[32,512]{1,0:T(8,128)} %bitcast.15, f32[512,512]{1,0:T(8,128)} %inv.3, f32[512,1536]{1,0:T(8,128)} %couple.7, s32[1,1536]{1,0:T(1,128)} %index.5, f32[16,32]{1,0:T(8,128)} %rhs_one.1, f32[16,4096]{1,0:T(8,128)} %inv_one.1), custom_call_target="tpu_custom_call" | custom-call | tf_op jit(solution)/shard_map/local_forward/pallas_call | solution.py:212
  6.2 0.0 copy-start.1
  6.2 11.2 %all-to-all-start = ((f32[64,24,128]{2,1,0:T(8,128)}), f32[64,24,128]{2,1,0:T(8,128)S(1)}, u32[]{:S(2)}, u32[]{:S(2)}) async-start(f32[64,24,128]{2,1,0:T(8,128)} %get-tuple-element.16), calls=%async_computation | async-start | bytes 1572864 | tf_op jit(solution)/shard_map/all_to_all | solution.py:482
  17.4 0.0 copy-done.4
  17.5 0.9 copy-done.2
  18.4 1.9 local_root.1
  20.3 11.1 %all-to-all-done.slots = f32[64,24,128]{2,1,0:T(8,128)S(1)} async-done(((f32[64,24,128]{2,1,0:T(8,128)}), f32[64,24,128]{2,1,0:T(8,128)S(1)}, u32[]{:S(2)}, u32[]{:S(2)}) %all-to-all-start) | async-done | bytes 786464 | tf_op jit(solution)/shard_map/all_to_all | solution.py:482
  31.4 0.1 slice_reduce_fusion
  31.5 18.3 %all_to_all.60.parts = f32[4,16,128]{2,1,0:T(8,128)S(1)} all-to-all(f32[4,16,128]{2,1,0:T(8,128)S(1)} %broadcast_in_dim.12), channel_id=1, replica_groups=mesh['half'=2,'pair'=4,'near'=2,'core'=2,'blk'=16] {'pair'}, dimensions={0} | all-to-all | bytes 65536 | tf_op jit(solution)/shard_map/all_to_all | solution.py:482
  49.8 0.6 solve_one.1
  50.4 15.9 %all_to_all.61.parts = f32[64,8,128]{2,1,0:T(8,128)S(1)} all-to-all(f32[64,8,128]{2,1,0:T(8,128)S(1)} %bitcast.10), channel_id=1, replica_groups=mesh['half'=2,'pair'=4,'near'=2,'core'=2,'blk'=16] {'near','core','blk'}, dimensions={0} | all-to-all | bytes 524288 | tf_op jit(solution)/shard_map/all_to_all | solution.py:482
  66.4 0.6 couple_up.1
  67.0 16.2 %all_to_all.62 = f32[64,16,128]{2,1,0:T(8,128)S(1)} all-to-all(f32[64,16,128]{2,1,0:T(8,128)S(1)} %get-tuple-element.23), channel_id=1, replica_groups=mesh['half'=2,'pair'=4,'near'=2,'core'=2,'blk'=16] {'near','core','blk'}, dimensions={0} | all-to-all | bytes 1048576 | tf_op jit(solution)/shard_map/all_to_all | solution.py:482
  83.2 0.1 reduce_sum.46
  83.3 20.0 %all_to_all.63.parts = f32[8,16,128]{2,1,0:T(8,128)S(1)} all-to-all(f32[8,16,128]{2,1,0:T(8,128)S(1)} %broadcast_in_dim.13), channel_id=1, replica_groups=mesh['half'=2,'pair'=4,'near'=2,'core'=2,'blk'=16] {'half','pair'}, dimensions={0} | all-to-all | bytes 131072 | tf_op jit(solution)/shard_map/all_to_all | solution.py:482
  103.2 0.5 solve_root.1
  103.7 14.4 %all_to_all.64 = f32[64,2,128]{2,1,0:T(2,128)S(1)} all-to-all(f32[64,2,128]{2,1,0:T(2,128)S(1)} %bitcast.13), channel_id=1, replica_groups=mesh['half'=2,'pair'=4,'near'=2,'core'=2,'blk'=16] {'near','core','blk'}, dimensions={0} | all-to-all | bytes 131072 | tf_op jit(solution)/shard_map/all_to_all | solution.py:482
  118.2 0.1 reduce_sum.47
  118.3 12.2 %all_to_all.65 = f32[64,2,128]{2,1,0:T(2,128)S(1)} all-to-all(f32[64,2,128]{2,1,0:T(2,128)S(1)} %broadcast_in_dim.14), channel_id=1, replica_groups=mesh['half'=2,'pair'=4,'near'=2,'core'=2,'blk'=16] {'near','core','blk'}, dimensions={0} | all-to-all | bytes 131072 | tf_op jit(solution)/shard_map/all_to_all | solution.py:482
  130.5 0.4 lift_root.1
  130.9 14.4 %all_to_all.66 = f32[8,16,128]{2,1,0:T(8,128)S(1)} all-to-all(f32[8,16,128]{2,1,0:T(8,128)S(1)} %lift_root.1), channel_id=1, replica_groups=mesh['half'=2,'pair'=4,'near'=2,'core'=2,'blk'=16] {'half','pair'}, dimensions={0} | all-to-all | bytes 131072 | tf_op jit(solution)/shard_map/all_to_all | solution.py:482
  145.4 17.6 %all_to_all.67.root = f32[64,16,128]{2,1,0:T(8,128)S(1)} all-to-all(f32[64,16,128]{2,1,0:T(8,128)S(1)} %broadcast_in_dim.15), channel_id=1, replica_groups=mesh['half'=2,'pair'=4,'near'=2,'core'=2,'blk'=16] {'near','core','blk'}, dimensions={0} | all-to-all | bytes 1048576 | tf_op jit(solution)/shard_map/all_to_all | solution.py:482
  163.1 0.4 rest_one.1
  163.5 13.4 %all_to_all.68 = f32[64,4,128]{2,1,0:T(4,128)S(1)} all-to-all(f32[64,4,128]{2,1,0:T(4,128)S(1)} %broadcast_in_dim.16), channel_id=1, replica_groups=mesh['half'=2,'pair'=4,'near'=2,'core'=2,'blk'=16] {'near','core','blk'}, dimensions={0} | all-to-all | bytes 262144 | tf_op jit(solution)/shard_map/all_to_all | solution.py:482
  176.9 0.5 lift_one.1
  177.4 10.8 %all_to_all.69 = f32[4,16,128]{2,1,0:T(8,128)S(1)} all-to-all(f32[4,16,128]{2,1,0:T(8,128)S(1)} %lift_one.1), channel_id=1, replica_groups=mesh['half'=2,'pair'=4,'near'=2,'core'=2,'blk'=16] {'pair'}, dimensions={0} | all-to-all | bytes 65536 | tf_op jit(solution)/shard_map/all_to_all | solution.py:482
  188.3 17.5 %all_to_all.70.one = f32[64,16,128]{2,1,0:T(8,128)} all-to-all(f32[64,16,128]{2,1,0:T(8,128)S(1)} %broadcast_in_dim.17), channel_id=1, replica_groups=mesh['half'=2,'pair'=4,'near'=2,'core'=2,'blk'=16] {'near','core','blk'}, dimensions={0} | all-to-all | bytes 1048576 | tf_op jit(solution)/shard_map/all_to_all | solution.py:482
  205.8 0.0 copy-done
  205.8 4.8 %local_backward.1 = (f32[32,512]{1,0:T(8,128)}, f32[16,32]{1,0:T(8,128)}, f32[8,32]{1,0:T(8,128)}) custom-call(f32[64,16,128]{2,1,0:T(8,128)} %all_to_all.70.one, f32[64,16,128]{2,1,0:T(8,128)} %copy-done, f32[32,512]{1,0:T(8,128)} %get-tuple-element.25.solved, f32[512,512]{1,0:T(8,128)} %inv.3, f32[512,1536]{1,0:T(8,128)} %couple.7, s32[1,1536]{1,0:T(1,128)} %index.5), custom_call_target="tpu_custom_call" | custom-call | tf_op jit(solution)/shard_map/local_backward/pallas_call | solution.py:336
  (13 shorter events, 0.2 us)
Async XLA Ops:
  0.6 16.8 %copy-start.4 = (s32[1,1536]{1,0:T(1,128)S(1)}, s32[1,1536]{1,0:T(1,128)}, u32[]{:S(2)}) copy-start(s32[1,1536]{1,0:T(1,128)} %index.5) | copy-start | bytes 18436
  0.6 16.8 %copy-start.3 = (f32[8,4096]{1,0:T(8,128)S(1)}, f32[8,4096]{1,0:T(8,128)}, u32[]{:S(2)}) copy-start(f32[8,4096]{1,0:T(8,128)} %inv_root.1) | copy-start | bytes 393220
  0.7 16.8 %copy-start.5 = (f32[8,32]{1,0:T(8,128)S(1)}, f32[8,32]{1,0:T(8,128)}, u32[]{:S(2)}) copy-start(f32[8,32]{1,0:T(8,128)} %rhs_root.1) | copy-start | bytes 3076
  6.2 60.1 %copy-start.1 = (f32[16,4096]{1,0:T(8,128)S(1)}, f32[16,4096]{1,0:T(8,128)}, u32[]{:S(2)}) copy-start(f32[16,4096]{1,0:T(8,128)} %couple.6) | copy-start | bytes 786436
  6.2 25.2 %all-to-all-start = ((f32[64,24,128]{2,1,0:T(8,128)}), f32[64,24,128]{2,1,0:T(8,128)S(1)}, u32[]{:S(2)}, u32[]{:S(2)}) async-start(f32[64,24,128]{2,1,0:T(8,128)} %get-tuple-element.16), calls=%async_computation | async-start | bytes 1572864 | tf_op jit(solution)/shard_map/all_to_all | solution.py:482
  17.5 0.9 copy-start.2
  163.1 42.7 %copy-start = (f32[64,16,128]{2,1,0:T(8,128)}, f32[64,16,128]{2,1,0:T(8,128)S(1)}, u32[]{:S(2)}) copy-start(f32[64,16,128]{2,1,0:T(8,128)S(1)} %all_to_all.67.root) | copy-start | bytes 1572868

commit v7 on v6

--- a/solution.py
+++ b/solution.py
@@ -311,13 +311,13 @@
     spread_rows(ancestor, 0, one_here)
     get_root.wait()
     spread_rows(ancestor, sep_rows, root_here)
-    here = position()
-    own_one[...] = own_rows(ancestor, here % (sep_rows // rows_one) * rows_one, rows_one)
-    own_root[...] = own_rows(ancestor, sep_rows + here * rows_root, rows_root)
     get_index.wait()
     gather_rows(above, ancestor, index_here, 0, index.shape[1] // WIDE)
     get_couple.wait()
     get_solved.wait()
+    here = position()
+    own_one[...] = own_rows(ancestor, here % (sep_rows // rows_one) * rows_one, rows_one)
+    own_root[...] = own_rows(ancestor, sep_rows + here * rows_root, rows_root)
     held = halves(above[...])
     both = jnp.concatenate(held, axis=1)
     rows = couple_here.shape[0] // 4

time: 211 us -> 211 us (level)
  no operation moved by 1% of the time
where the time goes in v7:
time: 211 us
  blocking collectives  171 us (81%)
  Pallas kernels  15.2 us (7%)
  starting transfers between devices  11.2 us (5%)
  waiting for transfers between devices  11.1 us (5%)
    all_to_all x11, blocking collectives, exchange(): return lax.all_to_all(slots, axes, 0, 0)  171 us
    all_to_all x1, starting transfers between devices, exchange(): return lax.all_to_all(slots, axes, 0, 0)  11.2 us
    all_to_all x1, waiting for transfers between devices, exchange(): return lax.all_to_all(slots, axes, 0, 0)  11.1 us
    pallas_call x1, Pallas kernels, forward(): pl.pallas_call(functools.partial(forward_kernel, position), out_shape=(ja...  5.55 us
    pallas_call x1, Pallas kernels, backward(): pl.pallas_call(functools.partial(backward_kernel, position), out_shape=(j...  4.75 us
  transfers between devices with their start and end apart: 1, of which 1 were waited for; matrix products, arithmetic and copies ran while one was open for 0% of the time, Pallas kernels for 1%

profile of v7, /device:TPU:1, one launch (start us, length us, event | category | flops | bytes accessed | tf_op | source)
XLA Modules:
  0.0 210.7 jit_solution(8539776365359799668)
XLA Ops:
  0.6 0.0 copy-start.4
  0.6 0.0 copy-start.3
  0.7 0.0 copy-start.5
  0.7 5.6 %local_forward.1 = (f32[64,24,128]{2,1,0:T(8,128)}, f32[32,512]{1,0:T(8,128)}, f32[32,1536]{1,0:T(8,128)}) custom-call(f32[32,512]{1,0:T(8,128)} %bitcast.15, f32[512,512]{1,0:T(8,128)} %inv.3, f32[512,1536]{1,0:T(8,128)} %couple.7, s32[1,1536]{1,0:T(1,128)} %index.5, f32[16,32]{1,0:T(8,128)} %rhs_one.1, f32[16,4096]{1,0:T(8,128)} %inv_one.1), custom_call_target="tpu_custom_call" | custom-call | tf_op jit(solution)/shard_map/local_forward/pallas_call | solution.py:212
  6.2 0.0 copy-start.1
  6.2 11.2 %all-to-all-start = ((f32[64,24,128]{2,1,0:T(8,128)}), f32[64,24,128]{2,1,0:T(8,128)S(1)}, u32[]{:S(2)}, u32[]{:S(2)}) async-start(f32[64,24,128]{2,1,0:T(8,128)} %get-tuple-element.16), calls=%async_computation | async-start | bytes 1572864 | tf_op jit(solution)/shard_map/all_to_all | solution.py:482
  17.5 0.0 copy-done.4
  17.5 0.0 copy-done.3
  17.5 0.9 copy-done.2
  18.4 1.9 local_root.1
  20.3 11.1 %all-to-all-done.slots = f32[64,24,128]{2,1,0:T(8,128)S(1)} async-done(((f32[64,24,128]{2,1,0:T(8,128)}), f32[64,24,128]{2,1,0:T(8,128)S(1)}, u32[]{:S(2)}, u32[]{:S(2)}) %all-to-all-start) | async-done | bytes 786464 | tf_op jit(solution)/shard_map/all_to_all | solution.py:482
  31.4 0.1 slice_reduce_fusion
  31.5 18.3 %all_to_all.60.parts = f32[4,16,128]{2,1,0:T(8,128)S(1)} all-to-all(f32[4,16,128]{2,1,0:T(8,128)S(1)} %broadcast_in_dim.12), channel_id=1, replica_groups=mesh['half'=2,'pair'=4,'near'=2,'core'=2,'blk'=16] {'pair'}, dimensions={0} | all-to-all | bytes 65536 | tf_op jit(solution)/shard_map/all_to_all | solution.py:482
  49.9 0.6 solve_one.1
  50.4 15.9 %all_to_all.61.parts = f32[64,8,128]{2,1,0:T(8,128)S(1)} all-to-all(f32[64,8,128]{2,1,0:T(8,128)S(1)} %bitcast.10), channel_id=1, replica_groups=mesh['half'=2,'pair'=4,'near'=2,'core'=2,'blk'=16] {'near','core','blk'}, dimensions={0} | all-to-all | bytes 524288 | tf_op jit(solution)/shard_map/all_to_all | solution.py:482
  66.4 0.6 couple_up.1
  67.0 16.2 %all_to_all.62 = f32[64,16,128]{2,1,0:T(8,128)S(1)} all-to-all(f32[64,16,128]{2,1,0:T(8,128)S(1)} %get-tuple-element.23), channel_id=1, replica_groups=mesh['half'=2,'pair'=4,'near'=2,'core'=2,'blk'=16] {'near','core','blk'}, dimensions={0} | all-to-all | bytes 1048576 | tf_op jit(solution)/shard_map/all_to_all | solution.py:482
  83.2 0.1 reduce_sum.46
  83.3 20.0 %all_to_all.63.parts = f32[8,16,128]{2,1,0:T(8,128)S(1)} all-to-all(f32[8,16,128]{2,1,0:T(8,128)S(1)} %broadcast_in_dim.13), channel_id=1, replica_groups=mesh['half'=2,'pair'=4,'near'=2,'core'=2,'blk'=16] {'half','pair'}, dimensions={0} | all-to-all | bytes 131072 | tf_op jit(solution)/shard_map/all_to_all | solution.py:482
  103.3 0.5 solve_root.1
  103.8 14.4 %all_to_all.64 = f32[64,2,128]{2,1,0:T(2,128)S(1)} all-to-all(f32[64,2,128]{2,1,0:T(2,128)S(1)} %bitcast.13), channel_id=1, replica_groups=mesh['half'=2,'pair'=4,'near'=2,'core'=2,'blk'=16] {'near','core','blk'}, dimensions={0} | all-to-all | bytes 131072 | tf_op jit(solution)/shard_map/all_to_all | solution.py:482
  118.2 0.1 reduce_sum.47
  118.3 12.2 %all_to_all.65 = f32[64,2,128]{2,1,0:T(2,128)S(1)} all-to-all(f32[64,2,128]{2,1,0:T(2,128)S(1)} %broadcast_in_dim.14), channel_id=1, replica_groups=mesh['half'=2,'pair'=4,'near'=2,'core'=2,'blk'=16] {'near','core','blk'}, dimensions={0} | all-to-all | bytes 131072 | tf_op jit(solution)/shard_map/all_to_all | solution.py:482
  130.5 0.4 lift_root.1
  131.0 14.4 %all_to_all.66 = f32[8,16,128]{2,1,0:T(8,128)S(1)} all-to-all(f32[8,16,128]{2,1,0:T(8,128)S(1)} %lift_root.1), channel_id=1, replica_groups=mesh['half'=2,'pair'=4,'near'=2,'core'=2,'blk'=16] {'half','pair'}, dimensions={0} | all-to-all | bytes 131072 | tf_op jit(solution)/shard_map/all_to_all | solution.py:482
  145.5 17.6 %all_to_all.67.root = f32[64,16,128]{2,1,0:T(8,128)S(1)} all-to-all(f32[64,16,128]{2,1,0:T(8,128)S(1)} %broadcast_in_dim.15), channel_id=1, replica_groups=mesh['half'=2,'pair'=4,'near'=2,'core'=2,'blk'=16] {'near','core','blk'}, dimensions={0} | all-to-all | bytes 1048576 | tf_op jit(solution)/shard_map/all_to_all | solution.py:482
  163.1 0.4 rest_one.1
  163.5 13.4 %all_to_all.68 = f32[64,4,128]{2,1,0:T(4,128)S(1)} all-to-all(f32[64,4,128]{2,1,0:T(4,128)S(1)} %broadcast_in_dim.16), channel_id=1, replica_groups=mesh['half'=2,'pair'=4,'near'=2,'core'=2,'blk'=16] {'near','core','blk'}, dimensions={0} | all-to-all | bytes 262144 | tf_op jit(solution)/shard_map/all_to_all | solution.py:482
  176.9 0.5 lift_one.1
  177.4 10.8 %all_to_all.69 = f32[4,16,128]{2,1,0:T(8,128)S(1)} all-to-all(f32[4,16,128]{2,1,0:T(8,128)S(1)} %lift_one.1), channel_id=1, replica_groups=mesh['half'=2,'pair'=4,'near'=2,'core'=2,'blk'=16] {'pair'}, dimensions={0} | all-to-all | bytes 65536 | tf_op jit(solution)/shard_map/all_to_all | solution.py:482
  188.3 17.5 %all_to_all.70.one = f32[64,16,128]{2,1,0:T(8,128)} all-to-all(f32[64,16,128]{2,1,0:T(8,128)S(1)} %broadcast_in_dim.17), channel_id=1, replica_groups=mesh['half'=2,'pair'=4,'near'=2,'core'=2,'blk'=16] {'near','core','blk'}, dimensions={0} | all-to-all | bytes 1048576 | tf_op jit(solution)/shard_map/all_to_all | solution.py:482
  205.8 4.7 %local_backward.1 = (f32[32,512]{1,0:T(8,128)}, f32[16,32]{1,0:T(8,128)}, f32[8,32]{1,0:T(8,128)}) custom-call(f32[64,16,128]{2,1,0:T(8,128)} %all_to_all.70.one, f32[64,16,128]{2,1,0:T(8,128)} %copy-done, f32[32,512]{1,0:T(8,128)} %get-tuple-element.25.solved, f32[512,512]{1,0:T(8,128)} %inv.3, f32[512,1536]{1,0:T(8,128)} %couple.7, s32[1,1536]{1,0:T(1,128)} %index.5), custom_call_target="tpu_custom_call" | custom-call | tf_op jit(solution)/shard_map/local_backward/pallas_call | solution.py:336
  (13 shorter events, 0.2 us)
Async XLA Ops:
  0.6 16.8 %copy-start.4 = (s32[1,1536]{1,0:T(1,128)S(1)}, s32[1,1536]{1,0:T(1,128)}, u32[]{:S(2)}) copy-start(s32[1,1536]{1,0:T(1,128)} %index.5) | copy-start | bytes 18436
  0.6 16.8 %copy-start.3 = (f32[8,4096]{1,0:T(8,128)S(1)}, f32[8,4096]{1,0:T(8,128)}, u32[]{:S(2)}) copy-start(f32[8,4096]{1,0:T(8,128)} %inv_root.1) | copy-start | bytes 393220
  0.7 16.8 %copy-start.5 = (f32[8,32]{1,0:T(8,128)S(1)}, f32[8,32]{1,0:T(8,128)}, u32[]{:S(2)}) copy-start(f32[8,32]{1,0:T(8,128)} %rhs_root.1) | copy-start | bytes 3076
  6.2 60.2 %copy-start.1 = (f32[16,4096]{1,0:T(8,128)S(1)}, f32[16,4096]{1,0:T(8,128)}, u32[]{:S(2)}) copy-start(f32[16,4096]{1,0:T(8,128)} %couple.6) | copy-start | bytes 786436
  6.2 25.2 %all-to-all-start = ((f32[64,24,128]{2,1,0:T(8,128)}), f32[64,24,128]{2,1,0:T(8,128)S(1)}, u32[]{:S(2)}, u32[]{:S(2)}) async-start(f32[64,24,128]{2,1,0:T(8,128)} %get-tuple-element.16), calls=%async_computation | async-start | bytes 1572864 | tf_op jit(solution)/shard_map/all_to_all | solution.py:482
  17.5 0.9 copy-start.2
  163.1 42.7 %copy-start = (f32[64,16,128]{2,1,0:T(8,128)}, f32[64,16,128]{2,1,0:T(8,128)S(1)}, u32[]{:S(2)}) copy-start(f32[64,16,128]{2,1,0:T(8,128)S(1)} %all_to_all.67.root) | copy-start | bytes 1572868
